TPU v7x, 128 devices: a whole 4x4x4 slice. The times are simulated.
128 devices in a mesh: hst: 16 (over z, x), doc: 8 (over y, core).
Axes of the slice: x: 4, y: 4, z: 4, core: 2. Of those that a mesh axis runs over, the one named last changes fastest.
Arguments:
- docs: bfloat16 [1048576, 768], P(('hst', 'doc')), may hold values from -400 to 400, as said below
- w_in: bfloat16 [768, 256], replicated, may hold values from -0.21875 to 0.21875
- w_out: bfloat16 [256, 64], replicated, may hold values from -0.375 to 0.375
- doc_host: int32 [1048576], P(('hst', 'doc')), may hold values from 0 to 2047
- tiles: bfloat16 [8192, 128, 128], P(('hst', 'doc')), may hold values from 0 to 10, as said below
- dst_block: int32 [8192], P(('hst', 'doc')), may hold values from 0 to 15
- src_block: int32 [8192], P(('hst', 'doc')), may hold values from 0 to 255
- tile_count: int32 [128], P(('hst', 'doc')), may hold values from 1 to 64, as said below
- teleport: int32 [32768], P('hst'), may hold values 0 or 1
Outputs:
- scores: float32 [32768, 64], P(('hst', 'doc'))
Inputs may be any that keep to these rules, and one draw needn't show every extreme that they name: `docs`: embeddings stay in the stated range. `tiles`: link weights are nonnegative. `tile_count`: some device uses all 64 slots.
All inputs are finite; a program needn't handle non-finite values. No bound on the sum of `teleport` on one device may be relied on, other than what follows from the above.
Results may differ from a plain program's by a relative error of at most 0.00066.
Values may be sent and summed in bfloat16 or wider, within the bound.
A program may use at most 128 MiB of HBM per device.

v0:
```python
import jax
import jax.numpy as jnp
from jax import lax
from jax.sharding import PartitionSpec as P

HOPS = 3


def body(docs, w_in, w_out, doc_host, tiles, dst_block, src_block, tile_count, teleport):
    host_dev = teleport.shape[0]
    block = tiles.shape[1]
    topics = w_out.shape[1]
    slots = tiles.shape[0]
    hosts_all = host_dev * lax.axis_size("hst")
    nblocks = hosts_all // block
    hidden = jax.nn.gelu(
        jnp.dot(docs, w_in, preferred_element_type=jnp.float32), approximate=True
    ).astype(jnp.bfloat16)
    probs = jax.nn.softmax(jnp.dot(hidden, w_out, preferred_element_type=jnp.float32), axis=-1)
    local_topic = jax.ops.segment_sum(probs, doc_host, num_segments=host_dev)
    used = (jnp.arange(slots) < tile_count[0]).astype(jnp.float32)
    colsum = jnp.sum(tiles, axis=1, dtype=jnp.float32)
    src_onehot = (src_block[:, None] == jnp.arange(nblocks)[None, :]).astype(jnp.float32) * used[
        :, None
    ]
    degree_blocks = jnp.dot(src_onehot.T, colsum, precision=lax.Precision.HIGHEST)
    degree = lax.psum(degree_blocks, ("hst", "doc")).reshape(hosts_all)
    own_degree = lax.dynamic_slice_in_dim(degree, lax.axis_index("hst") * host_dev, host_dev)
    inverse = 1.0 / jnp.maximum(own_degree, 1.0)
    dst_onehot = (dst_block[:, None] == jnp.arange(host_dev // block)[None, :]).astype(
        jnp.float32
    ) * used[:, None]
    member = teleport.astype(jnp.float32)
    rows = host_dev // lax.axis_size("doc")
    host_topic = lax.psum(local_topic, "doc")
    mass = lax.psum(jnp.sum(member[:, None] * host_topic, axis=0), "hst")
    tele = member[:, None] * host_topic / mass
    state = tele
    for hop in range(HOPS):
        sent = (state * inverse[:, None]).astype(jnp.bfloat16)
        full = lax.all_gather(sent, "hst", axis=0, tiled=True)
        slabs = full.reshape(nblocks, block, topics)[src_block]
        prod = jnp.einsum("kij,kjt->kit", tiles, slabs, preferred_element_type=jnp.float32)
        gathered = jnp.einsum("kb,kit->bit", dst_onehot, prod, precision=lax.Precision.HIGHEST)
        inflow = lax.psum(gathered.reshape(host_dev, topics), "doc")
        state = 0.85 * inflow + 0.15 * tele
    result = lax.dynamic_slice_in_dim(state, lax.axis_index("doc") * rows, rows)
    return hosts_all * result


def solution(mesh):
    placed = (
        P(("hst", "doc"), None),
        P(),
        P(),
        P(("hst", "doc")),
        P(("hst", "doc"), None, None),
        P(("hst", "doc")),
        P(("hst", "doc")),
        P(("hst", "doc")),
        P("hst"),
    )
    return jax.shard_map(
        body, mesh=mesh, in_specs=placed, out_specs=P(("hst", "doc"), None), check_vma=False
    )
```

profile of v0, /device:TPU:1, one launch (start us, length us, event | category | flops | bytes accessed | tf_op | source)
XLA Modules:
  0.0 639.2 jit_solution(17008999515403632906)
XLA Ops:
  7.3 2.1 convert_reduce_fusion
  9.4 1.8 convolution_bitcast_fusion
  11.1 0.0 all-reduce.8.cloned.1.call-update
  11.2 0.0 all-reduce.6.cloned.1.call-start
  11.2 8.6 %fusion.48 = (f32[8192]{0:T(1024)S(1)}, f32[8192,64]{0,1:T(8,128)S(1)}) fusion(bf16[256,64]{0,1:T(8,128)(2,1)} %param.11, bf16[8192,768]{1,0:T(8,128)(2,1)} %param.9, bf16[768,256]{1,0:T(8,128)(2,1)S(1)} %copy-done), kind=kOutput, calls=%fused_computation.78 | convolution fusion | flops 3509051392 | bytes 15138816 | tf_op jit(solution)/shard_map/dot_general | solution.py:19
  19.9 1.3 copy-done.2
  21.2 0.3 fusion.17
  21.6 1.9 fusion.16
  23.5 2.7 copy.18
  26.2 44.5 %scatter_custom_fusion = f32[2048,64]{1,0:T(8,128)S(1)} fusion(s32[8192]{0:T(1024)} %param.12, f32[8192,64]{1,0:T(8,128)} %copy.18, f32[]{:T(128)} %constant.16.clone.1), kind=kCustom, calls=%fused_computation.37 | custom fusion | flops 524288 | bytes 524800 | tf_op jit(solution)/shard_map/scatter-add | solution.py:20
  70.8 1.1 copy.19
  71.9 0.0 all-gather.4.cloned.1.call-start
  72.0 83.5 %all-reduce.8.cloned.1.call-done = f32[32768]{0:T(1024)} async-done(((f32[32768]{0:T(1024)}), f32[32768]{0:T(1024)}) %all-reduce.8.cloned.1.call-update) | async-done | bytes 131088 | tf_op jit(solution)/shard_map/psum | solution.py:27
  155.4 0.7 maximum_divide_fusion
  156.1 57.8 %all-reduce.6.cloned.1.call-done = f32[2048,64]{0,1:T(8,128)} async-done(((f32[2048,64]{0,1:T(8,128)}), f32[2048,64]{0,1:T(8,128)}) %all-reduce.6.cloned.1.call-update) | async-done | bytes 524304 | tf_op jit(solution)/shard_map/psum | solution.py:35
  214.0 1.2 multiply_reduce_fusion
  215.1 33.5 %psum.43 = f32[64]{0:T(128)S(1)} all-reduce(f32[64]{0:T(128)S(1)} %multiply_reduce_fusion), channel_id=1, replica_groups=mesh['hst'=16,'doc'=8] {'hst'}, use_global_device_ids=true, to_apply=%region_5.0 | all-reduce | flops 64 | bytes 512 | tf_op jit(solution)/shard_map/psum | solution.py:36
  248.6 1.9 multiply_convert_fusion.2
  250.5 0.2 all-reduce.10.cloned.1.call-start
  250.7 0.6 pad_clamp_fusion
  251.3 53.8 %all-gather.4.cloned.1.call-done = bf16[32768,64]{0,1:T(8,128)(2,1)} async-done(((bf16[2048,64]{0,1:T(8,128)(2,1)}), bf16[32768,64]{0,1:T(8,128)(2,1)}) %all-gather.4.cloned.1.call-update) | async-done | bytes 4194320 | tf_op jit(solution)/shard_map/all_gather | solution.py:41
  305.2 5.4 copy_bitcast_fusion.2
  310.5 3.2 gather_fusion
  313.8 1.5 convolution_bitcast_fusion.3
  315.4 2.2 fusion.14
  317.6 1.0 copy.46
  318.6 0.0 all-gather.6.cloned.1.call-start
  318.6 58.5 %all-reduce.10.cloned.1.call-done = f32[2048,64]{0,1:T(8,128)} async-done(((f32[2048,64]{0,1:T(8,128)}), f32[2048,64]{0,1:T(8,128)}) %all-reduce.10.cloned.1.call-update) | async-done | bytes 524304 | tf_op jit(solution)/shard_map/psum | solution.py:45
  377.1 2.2 multiply_convert_fusion.1
  379.3 0.0 all-reduce.12.cloned.1.call-start
  379.3 53.0 %all-gather.6.cloned.1.call-done = bf16[32768,64]{0,1:T(8,128)(2,1)} async-done(((bf16[2048,64]{0,1:T(8,128)(2,1)}), bf16[32768,64]{0,1:T(8,128)(2,1)}) %all-gather.6.cloned.1.call-update) | async-done | bytes 4194320 | tf_op jit(solution)/shard_map/all_gather | solution.py:41
  432.4 5.4 copy_bitcast_fusion.1
  437.7 3.1 gather_fusion.1
  440.8 1.5 convolution_bitcast_fusion.2
  442.4 2.2 fusion.12
  444.6 1.0 copy.45
  445.6 0.0 all-gather.8.cloned.1.call-start
  445.6 58.4 %all-reduce.12.cloned.1.call-done = f32[2048,64]{0,1:T(8,128)} async-done(((f32[2048,64]{0,1:T(8,128)}), f32[2048,64]{0,1:T(8,128)}) %all-reduce.12.cloned.1.call-update) | async-done | bytes 524304 | tf_op jit(solution)/shard_map/psum | solution.py:45
  504.1 1.8 multiply_convert_fusion
  505.9 0.3 all-reduce.14.cloned.1.call-start
  506.2 53.0 %all-gather.8.cloned.1.call-done = bf16[32768,64]{0,1:T(8,128)(2,1)} async-done(((bf16[2048,64]{0,1:T(8,128)(2,1)}), bf16[32768,64]{0,1:T(8,128)(2,1)}) %all-gather.8.cloned.1.call-update) | async-done | bytes 4194320 | tf_op jit(solution)/shard_map/all_gather | solution.py:41
  559.2 5.4 copy_bitcast_fusion
  564.5 3.1 gather_fusion.2
  567.6 1.5 convolution_bitcast_fusion.1
  569.1 2.2 fusion.10
  571.4 1.0 copy.44
  572.4 58.5 %all-reduce.14.cloned.1.call-done = f32[2048,64]{0,1:T(8,128)} async-done(((f32[2048,64]{0,1:T(8,128)}), f32[2048,64]{0,1:T(8,128)}) %all-reduce.14.cloned.1.call-update) | async-done | bytes 524304 | tf_op jit(solution)/shard_map/psum | solution.py:45
  630.8 1.5 fusion.20
  (38 shorter events, 0.2 us)
Async XLA Ops:
  6.5 4.7 copy-start
  6.5 148.9 %all-reduce.8.cloned.1.call-start = ((), (), s32[]{:S(2)}) async-start(), calls=%async_computation.1 | async-start | bytes 262144 | tf_op jit(solution)/shard_map/psum | solution.py:27
  7.3 2.1 copy-start.5
  11.2 202.8 %all-reduce.6.cloned.1.call-start = ((), (), s32[]{:S(2)}) async-start(), calls=%async_computation | async-start | bytes 1048576 | tf_op jit(solution)/shard_map/psum | solution.py:35
  19.9 1.3 copy-start.2
  23.5 48.5 %copy-start.8 = (s32[2048]{0:T(1024)S(1)}, s32[2048]{0:T(1024)}, u32[]{:S(2)}) copy-start(s32[2048]{0:T(1024)} %param.17) | copy-start | bytes 24580
  23.5 227.2 %copy-start.13 = (s32[64]{0:T(128)S(1)}, s32[64]{0:T(128)}, u32[]{:S(2)}) copy-start(s32[64]{0:T(128)} %param.15) | copy-start | bytes 772
  71.9 233.2 %all-gather.4.cloned.1.call-start = ((), (), s32[]{:S(2)}) async-start(), calls=%async_computation.2 | async-start | bytes 4456448 | tf_op jit(solution)/shard_map/all_gather | solution.py:41
  248.6 56.6 %copy-start.11 = (f32[64]{0:T(128)}, f32[64]{0:T(128)S(1)}, u32[]{:S(2)}) copy-start(f32[64]{0:T(128)S(1)} %psum.43) | copy-start | bytes 772
  250.5 126.6 %all-reduce.10.cloned.1.call-start = ((), (), s32[]{:S(2)}) async-start(), calls=%async_computation.3 | async-start | bytes 1048576 | tf_op jit(solution)/shard_map/psum | solution.py:45
  310.5 3.2 copy-start.1
  313.8 1.6 copy-start.6
  313.8 1.6 copy-start.9
  315.3 61.7 %copy-start.3 = (f32[2048,64]{0,1:T(8,128)S(1)}, f32[2048,64]{0,1:T(8,128)}, u32[]{:S(2)}) copy-start(f32[2048,64]{0,1:T(8,128)} %all-reduce.6.cloned.1.call-done) | copy-start | bytes 1572868
  315.3 61.7 %copy-start.12 = (f32[64]{0:T(128)S(1)}, f32[64]{0:T(128)}, u32[]{:S(2)}) copy-start(f32[64]{0:T(128)} %copy-done.11) | copy-start | bytes 772
  318.6 113.8 %all-gather.6.cloned.1.call-start = ((), (), s32[]{:S(2)}) async-start(), calls=%async_computation.4 | async-start | bytes 4456448 | tf_op jit(solution)/shard_map/all_gather | solution.py:41
  379.3 124.8 %all-reduce.12.cloned.1.call-start = ((), (), s32[]{:S(2)}) async-start(), calls=%async_computation.5 | async-start | bytes 1048576 | tf_op jit(solution)/shard_map/psum | solution.py:45
  437.7 4.6 copy-start.7
  437.7 4.6 copy-start.10
  442.4 61.7 %copy-start.4 = (f32[2048,64]{0,1:T(8,128)S(1)}, f32[2048,64]{0,1:T(8,128)}, u32[]{:S(2)}) copy-start(f32[2048,64]{0,1:T(8,128)} %get-tuple-element.6) | copy-start | bytes 1572868
  445.6 113.6 %all-gather.8.cloned.1.call-start = ((), (), s32[]{:S(2)}) async-start(), calls=%async_computation.6 | async-start | bytes 4456448 | tf_op jit(solution)/shard_map/all_gather | solution.py:41
  505.9 124.9 %all-reduce.14.cloned.1.call-start = ((), (), s32[]{:S(2)}) async-start(), calls=%async_computation.7 | async-start | bytes 1048576 | tf_op jit(solution)/shard_map/psum | solution.py:45
Sparse Core Ops, SparseCore 0:
  12.1 143.2 all-reduce.7
  157.9 56.0 all-reduce.5
  250.6 54.4 all-gather.3
  318.7 58.3 all-reduce.9
  379.4 52.9 all-gather.5
  445.7 58.2 all-reduce.11
  506.2 52.9 all-gather.7
  572.5 58.3 all-reduce.13
where the time goes:
time: 641 us; the launch traced here: 639 us
  waiting for transfers between devices  477 us (74%)
  other arithmetic  58.8 us (9%)
  local copies, waits for them, and re-layouts  33.6 us (5%)
  blocking collectives  33.5 us (5%)
  matrix products  21.7 us (3%)
  between operations  14.4 us (2%)
    psum x3, waiting for transfers between devices, body(): inflow = lax.psum(gathered.reshape(host_dev, topics), 'doc')  175 us
    all_gather x3, waiting for transfers between devices, body(): full = lax.all_gather(sent, 'hst', axis=0, tiled=True)  160 us
    psum x1, waiting for transfers between devices, body(): degree = lax.psum(degree_blocks, ('hst', 'doc')).reshape(hosts_all)  83.5 us
    psum x1, waiting for transfers between devices, body(): host_topic = lax.psum(local_topic, 'doc')  57.8 us
    scatter-add x1, other arithmetic, body(): local_topic = jax.ops.segment_sum(probs, doc_host, num_segments=host_dev)  44.5 us
    psum x1, blocking collectives, body(): mass = lax.psum(jnp.sum(member[:, None] * host_topic, axis=0), 'hst')  33.5 us
    reshape x3, local copies, waits for them, and re-layouts, body(): slabs = full.reshape(nblocks, block, topics)[src_block]  16.1 us
  transfers between devices with their start and end apart: 8, of which 8 were waited for; matrix products, arithmetic and copies ran while one was open for 9% of the time, Pallas kernels for 0%

commit v1 on v0

v1 whole, which is shorter than its diff:
```python
import functools
import jax
import jax.numpy as jnp
from jax import lax
from jax.experimental import pallas as pl
from jax.experimental.pallas import tpu as pltpu
from jax.sharding import PartitionSpec as P

HOPS = 3
MESH = pl.DeviceIdType.MESH
NT = (((1,), (1,)), ((), ()))


def local_kernel(
    dst_ref, src_ref, cnt_ref, docs_ref, win_ref, wout_ref, dh_ref, tiles_ref, tel_ref,
    lt_ref, stage_ref, meta_ref, acc_ref, colsum_ref,
):
    step = pl.program_id(0)
    steps = pl.num_programs(0)
    hosts = acc_ref.shape[0]
    topics = wout_ref.shape[1]
    slots = dst_ref.shape[0]
    nblk = lt_ref.shape[0]
    tiles_step = tiles_ref.shape[0]

    @pl.when(step == 0)
    def _():
        acc_ref[...] = jnp.zeros_like(acc_ref)
        stage_ref[...] = jnp.zeros_like(stage_ref)
        count = cnt_ref[0]

        def clear(i, carry):
            meta_ref[4, i] = 0
            return carry

        lax.fori_loop(0, nblk + 1, clear, 0)

        def tally(k, carry):
            key = jnp.where(k < count, dst_ref[k], nblk)
            meta_ref[4, key] = meta_ref[4, key] + 1
            return carry

        lax.fori_loop(0, slots, tally, 0)

        def spread(d, total):
            size = meta_ref[4, d]
            meta_ref[4, d] = total
            ends = total + size
            meta_ref[3, d] = jnp.maximum(ends - 1, 0)
            meta_ref[3, d + 32] = (size > 0).astype(jnp.int32)
            return ends

        lax.fori_loop(0, nblk + 1, spread, 0)

        def mark(k, carry):
            meta_ref[2, k] = 1
            return carry

        lax.fori_loop(0, slots, mark, 0)

        def first(d, carry):
            meta_ref[2, meta_ref[4, d]] = 0
            return carry

        lax.fori_loop(0, nblk + 1, first, 0)

        def place(k, carry):
            key = jnp.where(k < count, dst_ref[k], nblk)
            at = meta_ref[4, key]
            meta_ref[4, key] = at + 1
            meta_ref[0, at] = k
            meta_ref[1, at] = src_ref[k]
            return carry

        lax.fori_loop(0, slots, place, 0)

    hidden = jax.nn.gelu(
        jnp.dot(docs_ref[...], win_ref[...], preferred_element_type=jnp.float32), approximate=True
    ).astype(jnp.bfloat16)
    logits = jnp.dot(hidden, wout_ref[...], preferred_element_type=jnp.float32)
    weight = jnp.exp(logits - jnp.max(logits, axis=-1, keepdims=True))
    probs = weight / jnp.sum(weight, axis=-1, keepdims=True)
    high = probs.astype(jnp.bfloat16)
    low = (probs - high.astype(jnp.float32)).astype(jnp.bfloat16)
    both = jnp.concatenate([high, low], axis=1)
    owner = dh_ref[0]
    piece = 256
    for at in range(0, hosts, piece):
        row = lax.broadcasted_iota(jnp.int32, (piece, owner.shape[1]), 0) + at
        onehot = jnp.where(row == owner, 1.0, 0.0).astype(jnp.bfloat16)
        acc_ref[at : at + piece] += jnp.dot(onehot, both, preferred_element_type=jnp.float32)

    colsum_ref[...] = jnp.sum(tiles_ref[...].astype(jnp.float32), axis=1)
    for i in range(tiles_step):
        k = step * tiles_step + i
        used = jnp.where(k < cnt_ref[0], 1.0, 0.0)
        b = src_ref[k]
        row = (b // 4) * 8 + b % 4
        stage_ref[pl.ds(row, 1), :] += colsum_ref[i : i + 1, :] * used

    @pl.when(step == steps - 1)
    def _():
        mass = jnp.zeros((topics, 128), jnp.float32)
        for b in range(nblk):
            block = acc_ref[b * 128 : (b + 1) * 128]
            flat = jnp.transpose(block)
            flat = flat[:topics] + flat[topics:]
            lt_ref[b] = flat
            mass += flat * tel_ref[b : b + 1, :].astype(jnp.float32)
        wide = jnp.concatenate([mass, jnp.zeros_like(mass)], axis=0)
        mass_row = jnp.sum(jnp.transpose(wide), axis=0, keepdims=True)
        for j in range(stage_ref.shape[0] // 8):
            stage_ref[j * 8 + 4 : j * 8 + 5, :] = mass_row


def peer(dz, dx, dy, dc):
    h, d = lax.axis_index("hst"), lax.axis_index("doc")
    z = lax.rem(h // 4 + dz, 4)
    x = lax.rem(lax.rem(h, 4) + dx, 4)
    y = lax.rem(d // 2 + dy, 4)
    c = lax.rem(lax.rem(d, 2) + dc, 2)
    return (z * 4 + x, y * 2 + c)


PLANE = [(z, x, 0, 0) for z in range(4) for x in range(4) if z or x]
GROUP = [(0, 0, y, c) for y in range(4) for c in range(2) if y or c]
SIBLING = (0, 0, 0, 1)
ORDERS = (("x", "z", "y", 0, 3), ("z", "y", "x", 3, 3), ("y", "x", "z", 6, 2))


def net_kernel(
    meta_ref, lt_ref, stage_ref, meta_any, tiles_any, tel_ref, out_ref,
    own_tiles, sib_tiles, sib_meta, sib_smem, lt_in, stage_in, group_sum, group_in, part, rs_in,
    tele, state, all0, all1, all2, runs, final,
    loc_sem, sib_send, sib_recv, st_send, st_recv, gr_send, gr_recv, rs_send, rs_recv, ag_send, ag_recv,
):
    h, d = lax.axis_index("hst"), lax.axis_index("doc")
    pos = {"z": h // 4, "x": lax.rem(h, 4), "y": d // 2}
    core = lax.rem(d, 2)
    y = pos["y"]

    def remote(src, dst, send, recv, to):
        return pltpu.make_async_remote_copy(
            src_ref=src, dst_ref=dst, send_sem=send, recv_sem=recv, device_id=peer(*to), device_id_type=MESH
        )

    barrier = pltpu.get_barrier_semaphore()
    for to in PLANE + GROUP:
        pl.semaphore_signal(barrier, inc=1, device_id=peer(*to), device_id_type=MESH)
    pl.semaphore_wait(barrier, len(PLANE) + len(GROUP))

    mine = pl.multiple_of(core * 32, 32)
    other = pl.multiple_of(32 - core * 32, 32)
    lt_copy = remote(lt_ref.at[:, pl.ds(other, 32), :], lt_in, sib_send.at[0], sib_recv.at[0], SIBLING)
    lt_copy.start()
    stage_copies = []
    for j, to in enumerate(PLANE):
        there = peer(*to)[0]
        stage_copies.append(remote(stage_ref.at[there], stage_in.at[j], st_send.at[j], st_recv.at[j], to))
    for copy in stage_copies:
        copy.start()
    meta_copy = remote(meta_any, sib_meta, sib_send.at[1], sib_recv.at[1], SIBLING)
    meta_copy.start()
    tile_copy = remote(tiles_any, sib_tiles, sib_send.at[2], sib_recv.at[2], SIBLING)
    tile_copy.start()
    own_copy = pltpu.make_async_copy(tiles_any, own_tiles, loc_sem.at[0])
    own_copy.start()

    def reduce_start(inst):
        copies = []
        for k in range(1, 4):
            there = lax.rem(y + k, 4)
            copies.append(
                remote(
                    part.at[pl.ds(there * 4, 4)], rs_in.at[inst, k - 1],
                    rs_send.at[inst, k - 1], rs_recv.at[inst, k - 1], (0, 0, k, 0),
                )
            )
        for copy in copies:
            copy.start()
        return copies

    def reduce_end(inst, copies):
        for copy in copies:
            copy.wait_recv()
        total = part[pl.ds(y * 4, 4)] + rs_in[inst, 0] + rs_in[inst, 1] + rs_in[inst, 2]
        for copy in copies:
            copy.wait_send()
        return total

    lt_copy.wait()
    part[...] = lt_ref[:, pl.ds(mine, 32), :] + lt_in[...]
    copies = reduce_start(0)

    for copy in stage_copies:
        copy.wait_recv()
    total = stage_ref[h]
    for j in range(len(PLANE)):
        total += stage_in[j]
    group_sum[...] = total
    group_copies = []
    for j, to in enumerate(GROUP):
        there = peer(*to)[1] // 2
        group_copies.append(remote(group_sum.at[there], group_in.at[j], gr_send.at[j], gr_recv.at[j], to))
    for copy in group_copies:
        copy.start()
    for copy in stage_copies:
        copy.wait_send()
    meta_copy.wait()
    meta_local = pltpu.make_async_copy(sib_meta, sib_smem, loc_sem.at[1])
    meta_local.start()

    topic = reduce_end(0, copies)
    for copy in group_copies:
        copy.wait_recv()
    total = group_sum[y]
    for j in range(len(GROUP)):
        total += group_in[j]
    for copy in group_copies:
        copy.wait_send()
    inverse = (1.0 / jnp.maximum(total[0:4], 1.0))[:, None, :]
    square = jnp.transpose(jnp.broadcast_to(total[4:5], (128, 128)))
    mass = jnp.where(core == 0, square[0:32], square[32:64])
    member = tel_ref[pl.ds(y * 4, 4), :].astype(jnp.float32)[:, None, :]
    start = member * topic / mass[None]
    tele[...] = start
    state[...] = start
    meta_local.wait()
    own_copy.wait()
    tile_copy.wait()

    def hop_body(hop, gathered):
        def place(fixed, first, count):
            index = [fixed[axis] if axis in fixed else slice(None) for axis in "zxy"]
            return gathered.at[(*index, pl.ds(first, count))]

        sent = (state[...] * inverse).astype(jnp.bfloat16)
        gathered[pos["z"], pos["x"], y] = sent.reshape(8, 16, 128)
        started = []

        def along(axis, k):
            return tuple(k if axis == name else 0 for name in "zxy") + (0,)

        def send(o, slot, axis, k, ref):
            copy = remote(ref, ref, ag_send.at[hop, o, slot], ag_recv.at[hop, o, slot], along(axis, k))
            copy.start()
            started.append(copy)
            return copy

        one = []
        for o, (a1, a2, a3, first, count) in enumerate(ORDERS):
            ref = place(pos, first, count)
            one.append([send(o, k - 1, a1, k, ref) for k in range(1, 4)])
        two, three = [], []
        for o, (a1, a2, a3, first, count) in enumerate(ORDERS):
            for copy in one[o]:
                copy.wait_recv()
            ref = place({a2: pos[a2], a3: pos[a3]}, first, count)
            two.append([send(o, 2 + k, a2, k, ref) for k in range(1, 4)])
            three += [send(o, 5 + k, a3, k, ref) for k in range(1, 4)]
        for k2 in range(1, 4):
            for o, (a1, a2, a3, first, count) in enumerate(ORDERS):
                two[o][k2 - 1].wait_recv()
                there = lax.rem(pos[a2] + 4 - k2, 4)
                ref = place({a2: there, a3: pos[a3]}, first, count)
                three += [send(o, 5 + 3 * k2 + k, a3, k, ref) for k in range(1, 4)]
        for copy in three:
            copy.wait_recv()

        lists = ((meta_ref, own_tiles), (sib_smem, sib_tiles))
        batch = 8

        def tile_body(i, run):
            run = list(run)
            for j in range(batch):
                r = i * batch + j
                for n, (m, t) in enumerate(lists):
                    b = m[1, r]
                    slab = gathered[b // 64, (b // 16) % 4, (b // 4) % 4, pl.ds((b % 4) * 2, 2)]
                    prod = lax.dot_general(
                        slab.reshape(32, 128), t[m[0, r]], NT, preferred_element_type=jnp.float32
                    )
                    run[n] = jnp.where(m[2, r] > 0, run[n], 0.0) + prod
                    runs[n, r] = run[n]
            return tuple(run)

        zero = jnp.zeros((32, 128), jnp.float32)
        lax.fori_loop(0, own_tiles.shape[0] // batch, tile_body, (zero, zero))
        for blk in range(16):
            value = zero
            for n, (m, t) in enumerate(lists):
                value += jnp.where(m[3, blk + 32] > 0, runs[n, m[3, blk]], 0.0)
            part[blk] = value
        inflow = reduce_end(hop + 1, reduce_start(hop + 1))
        state[...] = 0.85 * inflow + 0.15 * tele[...]
        for copy in started:
            copy.wait_send()

    for hop, gathered in enumerate((all0, all1, all2)):
        hop_body(hop, gathered)

    hosts_all = 128.0 * 256.0
    keep = pl.multiple_of(core * 2, 2)
    give = pl.multiple_of(2 - core * 2, 2)
    state[...] = hosts_all * state[...]
    last = remote(
        state.at[pl.ds(give, 2)], final.at[:, pl.ds(mine, 32), :], sib_send.at[3], sib_recv.at[3], SIBLING
    )
    last.start()
    final[:, pl.ds(mine, 32), :] = state[pl.ds(keep, 2)]
    last.wait()
    for j in range(2):
        out_ref[j * 128 : (j + 1) * 128, :] = jnp.transpose(final[j])


def body(docs, w_in, w_out, doc_host, tiles, dst_block, src_block, tile_count, teleport):
    f32, bf16, i32 = jnp.float32, jnp.bfloat16, jnp.int32
    docs_dev, depth = docs.shape
    hidden, topics = w_out.shape
    slots = tiles.shape[0]
    hosts = teleport.shape[0]
    steps = 8
    rows = docs_dev // steps
    smem = pl.BlockSpec(memory_space=pltpu.SMEM)
    vmem = pl.BlockSpec(memory_space=pltpu.VMEM)
    anyw = pl.BlockSpec(memory_space=pl.ANY)
    member = teleport.reshape(16, 128)
    local_topic, stage, meta = pl.pallas_call(
        local_kernel,
        grid=(steps,),
        out_shape=(
            jax.ShapeDtypeStruct((16, topics, 128), f32),
            jax.ShapeDtypeStruct((512, 128), f32),
            jax.ShapeDtypeStruct((8, 128), i32),
        ),
        in_specs=[
            smem, smem, smem,
            pl.BlockSpec((rows, depth), lambda i: (i, 0)),
            pl.BlockSpec((depth, hidden), lambda i: (0, 0)),
            pl.BlockSpec((hidden, topics), lambda i: (0, 0)),
            pl.BlockSpec((1, 1, rows), lambda i: (i, 0, 0)),
            pl.BlockSpec((slots // steps, 128, 128), lambda i: (i, 0, 0)),
            pl.BlockSpec((16, 128), lambda i: (0, 0)),
        ],
        out_specs=(
            pl.BlockSpec((16, topics, 128), lambda i: (0, 0, 0)),
            pl.BlockSpec((512, 128), lambda i: (0, 0)),
            smem,
        ),
        scratch_shapes=[pltpu.VMEM((hosts, 128), f32), pltpu.VMEM((slots // steps, 128), f32)],
        compiler_params=pltpu.CompilerParams(vmem_limit_bytes=56 << 20),
        name="classify",
    )(
        dst_block, src_block, tile_count, docs, w_in, w_out,
        doc_host.reshape(steps, 1, rows), tiles, member,
    )
    dma = pltpu.SemaphoreType.DMA
    return pl.pallas_call(
        net_kernel,
        out_shape=jax.ShapeDtypeStruct((256, topics), f32),
        in_specs=[smem, vmem, vmem, anyw, anyw, vmem],
        out_specs=vmem,
        scratch_shapes=[
            pltpu.VMEM(tiles.shape, bf16),
            pltpu.VMEM(tiles.shape, bf16),
            pltpu.VMEM((8, 128), i32),
            pltpu.SMEM((8, 128), i32),
            pltpu.VMEM((16, 32, 128), f32),
            pltpu.VMEM((15, 4, 8, 128), f32),
            pltpu.VMEM((4, 8, 128), f32),
            pltpu.VMEM((7, 8, 128), f32),
            pltpu.VMEM((16, 32, 128), f32),
            pltpu.VMEM((HOPS + 1, 3, 4, 32, 128), f32),
            pltpu.VMEM((4, 32, 128), f32),
            pltpu.VMEM((4, 32, 128), f32),
            pltpu.VMEM((4, 4, 4, 8, 16, 128), bf16),
            pltpu.VMEM((4, 4, 4, 8, 16, 128), bf16),
            pltpu.VMEM((4, 4, 4, 8, 16, 128), bf16),
            pltpu.VMEM((2, slots, 32, 128), f32),
            pltpu.VMEM((2, 64, 128), f32),
            dma((2,)), dma((4,)), dma((4,)), dma((15,)), dma((15,)), dma((7,)), dma((7,)),
            dma((HOPS + 1, 3)), dma((HOPS + 1, 3)), dma((HOPS, 3, 18)), dma((HOPS, 3, 18)),
        ],
        compiler_params=pltpu.CompilerParams(
            collective_id=0, has_side_effects=True, vmem_limit_bytes=56 << 20
        ),
        name="spread",
    )(meta, local_topic, stage.reshape(16, 4, 8, 128), meta, tiles, member)


def solution(mesh):
    placed = (
        P(("hst", "doc"), None),
        P(),
        P(),
        P(("hst", "doc")),
        P(("hst", "doc"), None, None),
        P(("hst", "doc")),
        P(("hst", "doc")),
        P(("hst", "doc")),
        P("hst"),
    )
    return jax.shard_map(
        body, mesh=mesh, in_specs=placed, out_specs=P(("hst", "doc"), None), check_vma=False
    )
```

time: 641 us -> 136 us (0.21)
  waiting for transfers between devices: 477 us -> 0 us
  Pallas kernels: 0 us -> 132 us
  other arithmetic: 58.8 us -> 0 us
  blocking collectives: 33.5 us -> 0 us
  local copies, waits for them, and re-layouts: 33.6 us -> 3.11 us
  matrix products: 21.7 us -> 0 us
  between operations: 14.4 us -> 0.67 us
    psum x5 -> x0, waiting for transfers between devices: 317 us -> none  [the longest x3 175 us: body(): inflow = lax.psum(gathered.reshape(host_dev, topics), 'doc')]
    all_gather x3 -> x0, waiting for transfers between devices: 160 us -> none  [body(): full = lax.all_gather(sent, 'hst', axis=0, tiled=True)]
    pallas_call x0 -> x2, Pallas kernels: none -> 132 us  [the longest x1 101 us: body(): pl.pallas_call(net_kernel, out_shape=jax.ShapeDtypeStruct((256, topics),...]
    scatter-add x1 -> x0, other arithmetic: 44.5 us -> none  [body(): local_topic = jax.ops.segment_sum(probs, doc_host, num_segments=host_dev)]
    psum x1 -> x0, blocking collectives: 33.5 us -> none  [body(): mass = lax.psum(jnp.sum(member[:, None] * host_topic, axis=0), 'hst')]
    dot_general x8 -> x0, matrix products: 21.7 us -> none  [the longest x1 8.63 us: body(): jnp.dot(hidden, w_out, preferred_element_type=jnp.float32)]
    reshape x3 -> x0, local copies, waits for them, and re-layouts: 16.1 us -> none  [body(): slabs = full.reshape(nblocks, block, topics)[src_block]]
    gather x3 -> x0, local copies, waits for them, and re-layouts: 9.33 us -> none  [body(): slabs = full.reshape(nblocks, block, topics)[src_block]]
  transfers between devices with their start and end apart: 8 -> 0, of which waited for: 8 -> 0; matrix products, arithmetic and copies ran while one was open for 9% -> 0% of each run, Pallas kernels for 0% -> 0%
where the time goes in v1:
time: 136 us
  Pallas kernels  132 us (97%)
  local copies, waits for them, and re-layouts  3.11 us (2%)
    pallas_call x1, Pallas kernels, body(): pl.pallas_call(net_kernel, out_shape=jax.ShapeDtypeStruct((256, topics),...  101 us
    pallas_call x1, Pallas kernels, body(): pl.pallas_call(local_kernel, grid=(steps,), out_shape=(jax.ShapeDtypeStru...  31.8 us

profile of v1, /device:TPU:1, one launch (start us, length us, event | category | flops | bytes accessed | tf_op | source)
XLA Modules:
  0.0 136.1 jit_solution(12854677949244359363)
XLA Ops:
  0.7 1.5 %copy.10.wout_ref = bf16[256,64]{1,0:T(8,128)(2,1)} copy(bf16[256,64]{0,1:T(8,128)(2,1)} %param.11) | data formatting | bytes 65536 | tf_op args[2]
  2.1 31.8 %classify.1 = (f32[16,64,128]{2,1,0:T(8,128)}, f32[512,128]{1,0:T(8,128)}, s32[8,128]{1,0:T(8,128)}) custom-call(s32[64]{0:T(128)} %dst_ref.1, s32[64]{0:T(128)} %src_ref.1, s32[1]{0:T(128)S(6)} %copy.12.cnt_ref, bf16[8192,768]{1,0:T(8,128)(2,1)} %docs_ref.1, bf16[768,256]{1,0:T(8,128)(2,1)} %win_ref.1, bf16[256,64]{1,0:T(8,128)(2,1)} %copy.10.wout_ref, ...), custom_call_target="tpu_custom_call" | custom-call | tf_op jit(solution)/shard_map/classify/pallas_call | solution.py:328
  34.0 100.5 %spread.1 = f32[256,64]{1,0:T(8,128)} custom-call(s32[8,128]{1,0:T(8,128)} %get-tuple-element.8.meta_ref.meta_any, f32[16,64,128]{2,1,0:T(8,128)} %get-tuple-element.9.lt_ref, f32[16,4,8,128]{3,2,1,0:T(8,128)} %bitcast.3, s32[8,128]{1,0:T(8,128)} %get-tuple-element.8.meta_ref.meta_any, bf16[64,128,128]{2,1,0:T(8,128)(2,1)} %tiles_any.1, s32[16,128]{1,0:T(8,128)} %bitcast.6), custom_call_target="tpu_custom_call" | custom-call | tf_op jit(solution)/shard_map/spread/pallas_call | solution.py:358
  134.5 1.6 %copy.11 = f32[256,64]{0,1:T(8,128)} copy(f32[256,64]{1,0:T(8,128)} %spread.1) | data formatting | bytes 131072 | tf_op jit(solution)/shard_map/spread/pallas_call | solution.py:358

commit v2 on v1

--- a/solution.py
+++ b/solution.py
@@ -17,8 +17,7 @@
 ):
     step = pl.program_id(0)
     steps = pl.num_programs(0)
-    hosts = acc_ref.shape[0]
-    topics = wout_ref.shape[1]
+    topics = wout_ref.shape[0]
     slots = dst_ref.shape[0]
     nblk = lt_ref.shape[0]
     tiles_step = tiles_ref.shape[0]
@@ -74,22 +73,29 @@
 
         lax.fori_loop(0, slots, place, 0)
 
-    hidden = jax.nn.gelu(
-        jnp.dot(docs_ref[...], win_ref[...], preferred_element_type=jnp.float32), approximate=True
-    ).astype(jnp.bfloat16)
-    logits = jnp.dot(hidden, wout_ref[...], preferred_element_type=jnp.float32)
-    weight = jnp.exp(logits - jnp.max(logits, axis=-1, keepdims=True))
-    probs = weight / jnp.sum(weight, axis=-1, keepdims=True)
-    high = probs.astype(jnp.bfloat16)
-    low = (probs - high.astype(jnp.float32)).astype(jnp.bfloat16)
-    both = jnp.concatenate([high, low], axis=1)
+
     owner = dh_ref[0]
-    piece = 256
-    for at in range(0, hosts, piece):
-        row = lax.broadcasted_iota(jnp.int32, (piece, owner.shape[1]), 0) + at
-        onehot = jnp.where(row == owner, 1.0, 0.0).astype(jnp.bfloat16)
-        acc_ref[at : at + piece] += jnp.dot(onehot, both, preferred_element_type=jnp.float32)
-
+    upper = jnp.where(owner >= 1024, 1.0, 0.0).astype(jnp.bfloat16)
+    lower = jnp.where(owner >= 1024, 0.0, 1.0).astype(jnp.bfloat16)
+    pts = []
+    for c in range(0, docs_ref.shape[0], 1024):
+        hidden = jax.nn.gelu(
+            jnp.dot(docs_ref[c:c+1024], win_ref[...], preferred_element_type=jnp.float32), approximate=True
+        ).astype(jnp.bfloat16)
+        logits = lax.dot_general(wout_ref[...], hidden, NT, preferred_element_type=jnp.float32)
+        weight = jnp.exp(logits - jnp.max(logits, axis=0, keepdims=True))
+        probs = weight / jnp.sum(weight, axis=0, keepdims=True)
+        high = probs.astype(jnp.bfloat16)
+        low = (probs - high.astype(jnp.float32)).astype(jnp.bfloat16)
+        both = jnp.concatenate([high, low], axis=0)
+        pts.append(jnp.concatenate([both * lower[:, c:c+1024], both * upper[:, c:c+1024]], axis=0))
+    pt = jnp.concatenate(pts, axis=1)
+    spot = (owner & 1023)
+    piece = 512
+    for at in range(0, 1024, piece):
+        row = (lax.broadcasted_iota(jnp.int32, (piece, owner.shape[1]), 0) + at)
+        onehot = jnp.where(row == spot, 1.0, 0.0).astype(jnp.bfloat16)
+        acc_ref[at : at + piece] += lax.dot_general(onehot, pt, NT, preferred_element_type=jnp.float32)
     colsum_ref[...] = jnp.sum(tiles_ref[...].astype(jnp.float32), axis=1)
     for i in range(tiles_step):
         k = step * tiles_step + i
@@ -102,7 +108,7 @@
     def _():
         mass = jnp.zeros((topics, 128), jnp.float32)
         for b in range(nblk):
-            block = acc_ref[b * 128 : (b + 1) * 128]
+            block = acc_ref[b % 8 * 128 : (b % 8 + 1) * 128, b // 8 * 128 : (b // 8 + 1) * 128]
             flat = jnp.transpose(block)
             flat = flat[:topics] + flat[topics:]
             lt_ref[b] = flat
@@ -125,13 +131,17 @@
 PLANE = [(z, x, 0, 0) for z in range(4) for x in range(4) if z or x]
 GROUP = [(0, 0, y, c) for y in range(4) for c in range(2) if y or c]
 SIBLING = (0, 0, 0, 1)
-ORDERS = (("x", "z", "y", 0, 3), ("z", "y", "x", 3, 3), ("y", "x", "z", 6, 2))
+STREAMS = 2
+ORDERS = (
+    (("x", "z", "y", 0, 1), ("z", "y", "x", 1, 2), ("y", "x", "z", 3, 1)),
+    (("x", "z", "y", 0, 1), ("z", "y", "x", 1, 1), ("y", "x", "z", 2, 2)),
+)
 
 
 def net_kernel(
     meta_ref, lt_ref, stage_ref, meta_any, tiles_any, tel_ref, out_ref,
     own_tiles, sib_tiles, sib_meta, sib_smem, lt_in, stage_in, group_sum, group_in, part, rs_in,
-    tele, state, all0, all1, all2, runs, final,
+    tele, state, g00, g01, g10, g11, g20, g21, runs, final,
     loc_sem, sib_send, sib_recv, st_send, st_recv, gr_send, gr_recv, rs_send, rs_recv, ag_send, ag_recv,
 ):
     h, d = lax.axis_index("hst"), lax.axis_index("doc")
@@ -166,31 +176,34 @@
     own_copy = pltpu.make_async_copy(tiles_any, own_tiles, loc_sem.at[0])
     own_copy.start()
 
-    def reduce_start(inst):
+    def reduce_start(inst, s):
         copies = []
         for k in range(1, 4):
             there = lax.rem(y + k, 4)
             copies.append(
                 remote(
-                    part.at[pl.ds(there * 4, 4)], rs_in.at[inst, k - 1],
-                    rs_send.at[inst, k - 1], rs_recv.at[inst, k - 1], (0, 0, k, 0),
+                    part.at[s, pl.ds(there * 4, 4)], rs_in.at[inst, s, k - 1],
+                    rs_send.at[inst, s, k - 1], rs_recv.at[inst, s, k - 1], (0, 0, k, 0),
                 )
             )
         for copy in copies:
             copy.start()
         return copies
 
-    def reduce_end(inst, copies):
+    def reduce_end(inst, s, copies):
         for copy in copies:
             copy.wait_recv()
-        total = part[pl.ds(y * 4, 4)] + rs_in[inst, 0] + rs_in[inst, 1] + rs_in[inst, 2]
+        total = part[s, pl.ds(y * 4, 4)] + rs_in[inst, s, 0] + rs_in[inst, s, 1] + rs_in[inst, s, 2]
         for copy in copies:
             copy.wait_send()
         return total
 
     lt_copy.wait()
-    part[...] = lt_ref[:, pl.ds(mine, 32), :] + lt_in[...]
-    copies = reduce_start(0)
+    whole = lt_ref[:, pl.ds(mine, 32), :] + lt_in[...]
+    copies = []
+    for s in range(STREAMS):
+        part[s] = whole[:, s * 16 : s * 16 + 16]
+        copies.append(reduce_start(0, s))
 
     for copy in stage_copies:
         copy.wait_recv()
@@ -210,7 +223,7 @@
     meta_local = pltpu.make_async_copy(sib_meta, sib_smem, loc_sem.at[1])
     meta_local.start()
 
-    topic = reduce_end(0, copies)
+    topic = [reduce_end(0, s, copies[s]) for s in range(STREAMS)]
     for copy in group_copies:
         copy.wait_recv()
     total = group_sum[y]
@@ -222,95 +235,120 @@
     square = jnp.transpose(jnp.broadcast_to(total[4:5], (128, 128)))
     mass = jnp.where(core == 0, square[0:32], square[32:64])
     member = tel_ref[pl.ds(y * 4, 4), :].astype(jnp.float32)[:, None, :]
-    start = member * topic / mass[None]
-    tele[...] = start
-    state[...] = start
+    for s in range(STREAMS):
+        start = member * topic[s] / mass[None, s * 16 : s * 16 + 16]
+        tele[s] = start
+        state[s] = start
     meta_local.wait()
     own_copy.wait()
     tile_copy.wait()
 
-    def hop_body(hop, gathered):
-        def place(fixed, first, count):
+    def along(axis, k):
+        return tuple(k if axis == name else 0 for name in "zxy") + (0,)
+
+    class Stream:
+        def __init__(self, hop, s, gathered):
+            self.hop, self.s, self.gathered, self.started = hop, s, gathered, []
+
+        def place(self, fixed, first, count):
             index = [fixed[axis] if axis in fixed else slice(None) for axis in "zxy"]
-            return gathered.at[(*index, pl.ds(first, count))]
-
-        sent = (state[...] * inverse).astype(jnp.bfloat16)
-        gathered[pos["z"], pos["x"], y] = sent.reshape(8, 16, 128)
-        started = []
-
-        def along(axis, k):
-            return tuple(k if axis == name else 0 for name in "zxy") + (0,)
-
-        def send(o, slot, axis, k, ref):
-            copy = remote(ref, ref, ag_send.at[hop, o, slot], ag_recv.at[hop, o, slot], along(axis, k))
+            return self.gathered.at[(*index, pl.ds(first, count))]
+
+        def send(self, o, slot, axis, k, ref):
+            at = (self.hop, self.s, o, slot)
+            copy = remote(ref, ref, ag_send.at[at], ag_recv.at[at], along(axis, k))
             copy.start()
-            started.append(copy)
+            self.started.append(copy)
             return copy
 
-        one = []
-        for o, (a1, a2, a3, first, count) in enumerate(ORDERS):
-            ref = place(pos, first, count)
-            one.append([send(o, k - 1, a1, k, ref) for k in range(1, 4)])
-        two, three = [], []
-        for o, (a1, a2, a3, first, count) in enumerate(ORDERS):
-            for copy in one[o]:
+        def stage1(self):
+            sent = (state[self.s] * inverse).astype(jnp.bfloat16)
+            self.gathered[pos["z"], pos["x"], y] = sent
+            self.one = []
+            for o, (a1, a2, a3, first, count) in enumerate(ORDERS[self.s]):
+                ref = self.place(pos, first, count)
+                self.one.append([self.send(o, k - 1, a1, k, ref) for k in range(1, 4)])
+
+        def stage2(self):
+            self.two, self.three = [], []
+            for o, (a1, a2, a3, first, count) in enumerate(ORDERS[self.s]):
+                for copy in self.one[o]:
+                    copy.wait_recv()
+                ref = self.place({a2: pos[a2], a3: pos[a3]}, first, count)
+                self.two.append([self.send(o, 2 + k, a2, k, ref) for k in range(1, 4)])
+                self.three += [self.send(o, 5 + k, a3, k, ref) for k in range(1, 4)]
+
+        def stage3(self):
+            for k2 in (1, 3, 2):
+                for o, (a1, a2, a3, first, count) in enumerate(ORDERS[self.s]):
+                    self.two[o][k2 - 1].wait_recv()
+                    there = lax.rem(pos[a2] + 4 - k2, 4)
+                    ref = self.place({a2: there, a3: pos[a3]}, first, count)
+                    self.three += [self.send(o, 5 + 3 * k2 + k, a3, k, ref) for k in range(1, 4)]
+
+        def multiply(self):
+            for copy in self.three:
                 copy.wait_recv()
-            ref = place({a2: pos[a2], a3: pos[a3]}, first, count)
-            two.append([send(o, 2 + k, a2, k, ref) for k in range(1, 4)])
-            three += [send(o, 5 + k, a3, k, ref) for k in range(1, 4)]
-        for k2 in range(1, 4):
-            for o, (a1, a2, a3, first, count) in enumerate(ORDERS):
-                two[o][k2 - 1].wait_recv()
-                there = lax.rem(pos[a2] + 4 - k2, 4)
-                ref = place({a2: there, a3: pos[a3]}, first, count)
-                three += [send(o, 5 + 3 * k2 + k, a3, k, ref) for k in range(1, 4)]
-        for copy in three:
-            copy.wait_recv()
-
-        lists = ((meta_ref, own_tiles), (sib_smem, sib_tiles))
-        batch = 8
-
-        def tile_body(i, run):
-            run = list(run)
-            for j in range(batch):
-                r = i * batch + j
+            lists = ((meta_ref, own_tiles), (sib_smem, sib_tiles))
+            batch = 32
+            gathered, s = self.gathered, self.s
+
+            def tile_body(i, run):
+                run = list(run)
+                for j in range(batch):
+                    r = i * batch + j
+                    for n, (m, t) in enumerate(lists):
+                        b = m[1, r]
+                        slab = gathered[b // 64, (b // 16) % 4, (b // 4) % 4, b % 4]
+                        prod = lax.dot_general(slab, t[m[0, r]], NT, preferred_element_type=jnp.float32)
+                        run[n] = jnp.where(m[2, r] > 0, run[n], 0.0) + prod
+                        runs[n, r] = run[n]
+                return tuple(run)
+
+            zero = jnp.zeros((16, 128), jnp.float32)
+            lax.fori_loop(0, own_tiles.shape[0] // batch, tile_body, (zero, zero))
+            for blk in range(16):
+                value = zero
                 for n, (m, t) in enumerate(lists):
-                    b = m[1, r]
-                    slab = gathered[b // 64, (b // 16) % 4, (b // 4) % 4, pl.ds((b % 4) * 2, 2)]
-                    prod = lax.dot_general(
-                        slab.reshape(32, 128), t[m[0, r]], NT, preferred_element_type=jnp.float32
-                    )
-                    run[n] = jnp.where(m[2, r] > 0, run[n], 0.0) + prod
-                    runs[n, r] = run[n]
-            return tuple(run)
-
-        zero = jnp.zeros((32, 128), jnp.float32)
-        lax.fori_loop(0, own_tiles.shape[0] // batch, tile_body, (zero, zero))
-        for blk in range(16):
-            value = zero
-            for n, (m, t) in enumerate(lists):
-                value += jnp.where(m[3, blk + 32] > 0, runs[n, m[3, blk]], 0.0)
-            part[blk] = value
-        inflow = reduce_end(hop + 1, reduce_start(hop + 1))
-        state[...] = 0.85 * inflow + 0.15 * tele[...]
-        for copy in started:
-            copy.wait_send()
-
-    for hop, gathered in enumerate((all0, all1, all2)):
-        hop_body(hop, gathered)
+                    value += jnp.where(m[3, blk + 32] > 0, runs[n, m[3, blk]], 0.0)
+                part[s, blk] = value
+            self.reducing = reduce_start(self.hop + 1, s)
+
+        def finish(self):
+            inflow = reduce_end(self.hop + 1, self.s, self.reducing)
+            state[self.s] = 0.85 * inflow + 0.15 * tele[self.s]
+
+        def settle(self):
+            for copy in self.started:
+                copy.wait_send()
+
+    streams = [[Stream(hop, s, g) for s, g in enumerate(gs)] for hop, gs in enumerate(((g00, g01), (g10, g11), (g20, g21)))]
+    for one in streams[0]:
+        one.stage1()
+    for hop in range(HOPS):
+        for one in streams[hop]:
+            one.stage2()
+        for one in streams[hop]:
+            one.stage3()
+        for one in streams[hop]:
+            one.multiply()
+        for s, one in enumerate(streams[hop]):
+            one.finish()
+            if hop + 1 < HOPS:
+                streams[hop + 1][s].stage1()
+        for one in streams[hop]:
+            one.settle()
 
     hosts_all = 128.0 * 256.0
     keep = pl.multiple_of(core * 2, 2)
     give = pl.multiple_of(2 - core * 2, 2)
     state[...] = hosts_all * state[...]
-    last = remote(
-        state.at[pl.ds(give, 2)], final.at[:, pl.ds(mine, 32), :], sib_send.at[3], sib_recv.at[3], SIBLING
-    )
+    last = remote(state.at[:, pl.ds(give, 2)], final.at[core], sib_send.at[3], sib_recv.at[3], SIBLING)
     last.start()
-    final[:, pl.ds(mine, 32), :] = state[pl.ds(keep, 2)]
+    final[core] = state[:, pl.ds(keep, 2)]
     last.wait()
     for j in range(2):
-        out_ref[j * 128 : (j + 1) * 128, :] = jnp.transpose(final[j])
+        out_ref[j * 128 : (j + 1) * 128, :] = jnp.transpose(final[:, :, j].reshape(64, 128))
 
 
 def body(docs, w_in, w_out, doc_host, tiles, dst_block, src_block, tile_count, teleport):
@@ -337,7 +375,7 @@
             smem, smem, smem,
             pl.BlockSpec((rows, depth), lambda i: (i, 0)),
             pl.BlockSpec((depth, hidden), lambda i: (0, 0)),
-            pl.BlockSpec((hidden, topics), lambda i: (0, 0)),
+            pl.BlockSpec((topics, hidden), lambda i: (0, 0)),
             pl.BlockSpec((1, 1, rows), lambda i: (i, 0, 0)),
             pl.BlockSpec((slots // steps, 128, 128), lambda i: (i, 0, 0)),
             pl.BlockSpec((16, 128), lambda i: (0, 0)),
@@ -347,11 +385,11 @@
             pl.BlockSpec((512, 128), lambda i: (0, 0)),
             smem,
         ),
-        scratch_shapes=[pltpu.VMEM((hosts, 128), f32), pltpu.VMEM((slots // steps, 128), f32)],
+        scratch_shapes=[pltpu.VMEM((1024, 256), f32), pltpu.VMEM((slots // steps, 128), f32)],
         compiler_params=pltpu.CompilerParams(vmem_limit_bytes=56 << 20),
         name="classify",
     )(
-        dst_block, src_block, tile_count, docs, w_in, w_out,
+        dst_block, src_block, tile_count, docs, w_in, w_out.T,
         doc_host.reshape(steps, 1, rows), tiles, member,
     )
     dma = pltpu.SemaphoreType.DMA
@@ -369,17 +407,16 @@
             pltpu.VMEM((15, 4, 8, 128), f32),
             pltpu.VMEM((4, 8, 128), f32),
             pltpu.VMEM((7, 8, 128), f32),
-            pltpu.VMEM((16, 32, 128), f32),
-            pltpu.VMEM((HOPS + 1, 3, 4, 32, 128), f32),
-            pltpu.VMEM((4, 32, 128), f32),
-            pltpu.VMEM((4, 32, 128), f32),
-            pltpu.VMEM((4, 4, 4, 8, 16, 128), bf16),
-            pltpu.VMEM((4, 4, 4, 8, 16, 128), bf16),
-            pltpu.VMEM((4, 4, 4, 8, 16, 128), bf16),
-            pltpu.VMEM((2, slots, 32, 128), f32),
-            pltpu.VMEM((2, 64, 128), f32),
+            pltpu.VMEM((STREAMS, 16, 16, 128), f32),
+            pltpu.VMEM((HOPS + 1, STREAMS, 3, 4, 16, 128), f32),
+            pltpu.VMEM((STREAMS, 4, 16, 128), f32),
+            pltpu.VMEM((STREAMS, 4, 16, 128), f32),
+            *[pltpu.VMEM((4, 4, 4, 4, 16, 128), bf16) for _ in range(HOPS * STREAMS)],
+            pltpu.VMEM((2, slots, 16, 128), f32),
+            pltpu.VMEM((2, STREAMS, 2, 16, 128), f32),
             dma((2,)), dma((4,)), dma((4,)), dma((15,)), dma((15,)), dma((7,)), dma((7,)),
-            dma((HOPS + 1, 3)), dma((HOPS + 1, 3)), dma((HOPS, 3, 18)), dma((HOPS, 3, 18)),
+            dma((HOPS + 1, STREAMS, 3)), dma((HOPS + 1, STREAMS, 3)),
+            dma((HOPS, STREAMS, 3, 18)), dma((HOPS, STREAMS, 3, 18)),
         ],
         compiler_params=pltpu.CompilerParams(
             collective_id=0, has_side_effects=True, vmem_limit_bytes=56 << 20

time: 136 us -> 117 us (0.86)
  Pallas kernels: 132 us -> 114 us
  local copies, waits for them, and re-layouts: 3.11 us -> 1.62 us
    pallas_call x1, Pallas kernels: 31.8 us -> 18.7 us  [body(): pl.pallas_call(local_kernel, grid=(steps,), out_shape=(jax.ShapeDtypeStru...]
    pallas_call x1, Pallas kernels: 101 us -> 95.7 us  [body(): pl.pallas_call(net_kernel, out_shape=jax.ShapeDtypeStruct((256, topics),...]
    unnamed x1 -> x0, local copies, waits for them, and re-layouts: 1.49 us -> none
where the time goes in v2:
time: 117 us
  Pallas kernels  114 us (97%)
  local copies, waits for them, and re-layouts  1.62 us (1%)
    pallas_call x1, Pallas kernels, body(): pl.pallas_call(net_kernel, out_shape=jax.ShapeDtypeStruct((256, topics),...  95.7 us
    pallas_call x1, Pallas kernels, body(): pl.pallas_call(local_kernel, grid=(steps,), out_shape=(jax.ShapeDtypeStru...  18.7 us

profile of v2, /device:TPU:1, one launch (start us, length us, event | category | flops | bytes accessed | tf_op | source)
XLA Modules:
  0.0 116.7 jit_solution(9382464117895083032)
XLA Ops:
  0.7 18.7 %classify.1 = (f32[16,64,128]{2,1,0:T(8,128)}, f32[512,128]{1,0:T(8,128)}, s32[8,128]{1,0:T(8,128)}) custom-call(s32[64]{0:T(128)} %dst_ref.1, s32[64]{0:T(128)} %src_ref.1, s32[1]{0:T(128)S(6)} %copy.11.cnt_ref, bf16[8192,768]{1,0:T(8,128)(2,1)} %docs_ref.1, bf16[768,256]{1,0:T(8,128)(2,1)} %win_ref.1, bf16[64,256]{1,0:T(8,128)(2,1)} %bitcast.5, ...), custom_call_target="tpu_custom_call" | custom-call | tf_op jit(solution)/shard_map/classify/pallas_call | solution.py:366
  19.4 95.7 %spread.1 = f32[256,64]{1,0:T(8,128)} custom-call(s32[8,128]{1,0:T(8,128)} %get-tuple-element.8.meta_ref.meta_any, f32[16,64,128]{2,1,0:T(8,128)} %get-tuple-element.9.lt_ref, f32[16,4,8,128]{3,2,1,0:T(8,128)} %bitcast.4, s32[8,128]{1,0:T(8,128)} %get-tuple-element.8.meta_ref.meta_any, bf16[64,128,128]{2,1,0:T(8,128)(2,1)} %tiles_any.1, s32[16,128]{1,0:T(8,128)} %bitcast.8), custom_call_target="tpu_custom_call" | custom-call | tf_op jit(solution)/shard_map/spread/pallas_call | solution.py:396
  115.1 1.6 %copy.10 = f32[256,64]{0,1:T(8,128)} copy(f32[256,64]{1,0:T(8,128)} %spread.1) | data formatting | bytes 131072 | tf_op jit(solution)/shard_map/spread/pallas_call | solution.py:396

commit v3 on v0

v3 whole, which is shorter than its diff:
```python
import jax
import jax.numpy as jnp
from jax import lax
from jax.experimental import pallas as pl
from jax.experimental.pallas import tpu as pltpu
from jax.sharding import PartitionSpec as P

HOPS = 3
MESH = pl.DeviceIdType.MESH
NT = (((1,), (1,)), ((), ()))


def peer(dz, dx, dy, dc):
    h, d = lax.axis_index("hst"), lax.axis_index("doc")
    z = lax.rem(h // 4 + dz, 4)
    x = lax.rem(lax.rem(h, 4) + dx, 4)
    y = lax.rem(d // 2 + dy, 4)
    c = lax.rem(lax.rem(d, 2) + dc, 2)
    return (z * 4 + x, y * 2 + c)


PLANE = [(z, x, 0, 0) for z in range(4) for x in range(4) if z or x]
GROUP = [(0, 0, y, c) for y in range(4) for c in range(2) if y or c]
SIBLING = (0, 0, 0, 1)
STREAMS = 2
ORDERS = (
    (("x", "z", "y", 0, 1), ("z", "y", "x", 1, 2), ("y", "x", "z", 3, 1)),
    (("x", "z", "y", 0, 1), ("z", "y", "x", 1, 1), ("y", "x", "z", 2, 2)),
)


def order_tiles(dst_ref, src_ref, count, rows, meta):
    i32 = jnp.int32
    slots = dst_ref.shape[1]
    rows[...] = jnp.zeros_like(rows)
    rows[0:1, 0:slots] = dst_ref[...]
    rows[1:2, 0:slots] = src_ref[...]
    lane = lax.broadcasted_iota(i32, (128, 128), 1)
    sub = lax.broadcasted_iota(i32, (128, 128), 0)
    key = jnp.where(lane[0:1] < count, rows[0:1], jnp.where(lane[0:1] < slots, 16, 17))
    key_row = jnp.broadcast_to(key, (128, 128))
    key_col = jnp.transpose(key_row)
    src_col = jnp.transpose(jnp.broadcast_to(rows[1:2], (128, 128)))
    before = (key_row < key_col) | ((key_row == key_col) & (lane < sub))
    rank = jnp.sum(jnp.where(before, 1, 0), axis=1, keepdims=True)
    here = jnp.broadcast_to(rank, (128, 128)) == lane

    def down(value):
        return jnp.sum(value, axis=0, keepdims=True)

    perm = down(jnp.where(here, sub, 0))
    source = down(jnp.where(here, src_col, 0))
    sorted_key = down(jnp.where(here, key_col, 0))
    first = down(jnp.where(key_col < sorted_key, 1, 0))
    follows = jnp.where(lane[0:1] > first, 1, 0)
    upto = down(jnp.where(key_col <= lane, 1, 0))
    below = down(jnp.where(key_col < lane, 1, 0))
    some = jnp.where(upto > below, 1, 0)
    meta[0:1] = jnp.clip(perm, 0, slots - 1)
    meta[1:2] = jnp.clip(source, 0, 255)
    meta[2:3] = follows
    meta[3:4] = jnp.clip(upto - 1, 0, slots - 1)
    meta[4:5] = some


def split3(value):
    one = value.astype(jnp.bfloat16)
    rest = value - one.astype(jnp.float32)
    two = rest.astype(jnp.bfloat16)
    three = (rest - two.astype(jnp.float32)).astype(jnp.bfloat16)
    return one, two, three


def kernel(
    cnt_ref, dst_ref, src_ref, docs_ref, win_ref, wout_ref, dh_ref, tel_ref, tiles_any, out_ref,
    acc, lt, rows, meta, own_smem, sib_meta, sib_smem, own_tiles, sib_tiles, lt_in, stage, stage_in,
    group_sum, group_in, mass_own, mass_in, mass_sum, mass_all, part, rs_in,
    tele, state, g00, g01, g10, g11, g20, g21, runs, final,
    loc_sem, sib_send, sib_recv, st_send, st_recv, gr_send, gr_recv,
    ms_send, ms_recv, mg_send, mg_recv, rs_send, rs_recv, ag_send, ag_recv,
):
    step = pl.program_id(0)
    h, d = lax.axis_index("hst"), lax.axis_index("doc")
    pos = {"z": h // 4, "x": lax.rem(h, 4), "y": d // 2}
    core = lax.rem(d, 2)
    y = pos["y"]
    topics = wout_ref.shape[0]
    mine = pl.multiple_of(core * 32, 32)
    other = pl.multiple_of(32 - core * 32, 32)

    def remote(src, dst, send, recv, to):
        return pltpu.make_async_remote_copy(
            src_ref=src, dst_ref=dst, send_sem=send, recv_sem=recv, device_id=peer(*to), device_id_type=MESH
        )

    def wait_bytes(ref, sem):
        pltpu.make_async_copy(ref, ref, sem).wait()

    own_copy = pltpu.make_async_copy(tiles_any, own_tiles, loc_sem.at[0])
    meta_own = pltpu.make_async_copy(meta, own_smem, loc_sem.at[1])
    meta_local = pltpu.make_async_copy(sib_meta, sib_smem, loc_sem.at[2])
    meta_copy = remote(meta, sib_meta, sib_send.at[1], sib_recv.at[1], SIBLING)
    tile_copy = remote(own_tiles, sib_tiles, sib_send.at[2], sib_recv.at[2], SIBLING)
    stage_copies = [
        remote(stage.at[peer(*to)[0]], stage_in.at[j], st_send, st_recv, to)
        for j, to in enumerate(PLANE)
    ]
    group_copies = [
        remote(group_sum.at[peer(*to)[1] // 2], group_in.at[j], gr_send, gr_recv, to)
        for j, to in enumerate(GROUP)
    ]
    mass_copies = [
        remote(mass_own, mass_in.at[j], ms_send, ms_recv, to) for j, to in enumerate(PLANE)
    ]
    total_copies = [
        remote(mass_sum, mass_all.at[j], mg_send, mg_recv, to) for j, to in enumerate(GROUP)
    ]

    @pl.when(step == 0)
    def _():
        barrier = pltpu.get_barrier_semaphore()
        for to in PLANE + GROUP:
            pl.semaphore_signal(barrier, inc=1, device_id=peer(*to), device_id_type=MESH)
        own_copy.start()
        acc[...] = jnp.zeros_like(acc)
        order_tiles(dst_ref, src_ref, cnt_ref[0], rows, meta)
        meta_own.start()
        own_copy.wait()

    @pl.when(step == 2)
    def _():
        pl.semaphore_wait(pltpu.get_barrier_semaphore(), len(PLANE) + len(GROUP))
        meta_copy.start()
        tile_copy.start()
        slots = own_tiles.shape[0]
        colsum = jnp.sum(own_tiles[...].astype(jnp.float32), axis=1)
        row = lax.broadcasted_iota(jnp.int32, (512, slots), 0)
        src = src_ref[...]
        used = lax.broadcasted_iota(jnp.int32, (1, slots), 1) < cnt_ref[0]
        spot = jnp.where(used, (src // 4) * 8 + src % 4, 7)
        onehot = jnp.where(row == spot, 1.0, 0.0).astype(jnp.bfloat16)
        degree = sum(jnp.dot(onehot, p, preferred_element_type=jnp.float32) for p in split3(colsum))
        stage[...] = degree.reshape(16, 4, 8, 128)
        for copy in stage_copies:
            copy.start()

    @pl.when(step == 4)
    def _():
        wait_bytes(stage_in, st_recv)
        total = stage[h]
        for j in range(len(PLANE)):
            total += stage_in[j]
        group_sum[...] = total
        for copy in group_copies:
            copy.start()
        wait_bytes(stage_in, st_send)
        meta_copy.wait()
        meta_local.start()

    owner = dh_ref[0]
    upper = jnp.where(owner >= 1024, 1.0, 0.0).astype(jnp.bfloat16)
    lower = jnp.where(owner >= 1024, 0.0, 1.0).astype(jnp.bfloat16)
    pts = []
    for c in range(0, docs_ref.shape[0], 1024):
        hidden = jax.nn.gelu(
            jnp.dot(docs_ref[c:c+1024], win_ref[...], preferred_element_type=jnp.float32), approximate=True
        ).astype(jnp.bfloat16)
        logits = lax.dot_general(wout_ref[...], hidden, NT, preferred_element_type=jnp.float32)
        weight = jnp.exp(logits - jnp.max(logits, axis=0, keepdims=True))
        probs = weight / jnp.sum(weight, axis=0, keepdims=True)
        high = probs.astype(jnp.bfloat16)
        low = (probs - high.astype(jnp.float32)).astype(jnp.bfloat16)
        both = jnp.concatenate([high, low], axis=0)
        pts.append(jnp.concatenate([both * lower[:, c:c+1024], both * upper[:, c:c+1024]], axis=0))
    pt = jnp.concatenate(pts, axis=1)
    spot = (owner & 1023)
    piece = 512
    for at in range(0, 1024, piece):
        row = (lax.broadcasted_iota(jnp.int32, (piece, owner.shape[1]), 0) + at)
        onehot = jnp.where(row == spot, 1.0, 0.0).astype(jnp.bfloat16)
        acc[at : at + piece] += lax.dot_general(onehot, pt, NT, preferred_element_type=jnp.float32)

    @pl.when(step == pl.num_programs(0) - 1)
    def _():
        mass = jnp.zeros((topics, 128), jnp.float32)
        for b in range(16):
            flat = jnp.transpose(acc[b % 8 * 128 : (b % 8 + 1) * 128, b // 8 * 128 : (b // 8 + 1) * 128])
            flat = flat[:topics] + flat[topics:]
            lt[b] = flat
            mass += flat * tel_ref[b : b + 1, :].astype(jnp.float32)
        lt_copy = remote(lt.at[:, pl.ds(other, 32), :], lt_in, sib_send.at[0], sib_recv.at[0], SIBLING)
        lt_copy.start()
        wide = jnp.concatenate([mass, jnp.zeros_like(mass)], axis=0)
        mass_own[...] = jnp.broadcast_to(jnp.sum(jnp.transpose(wide), axis=0, keepdims=True), (8, 128))
        for copy in mass_copies:
            copy.start()
        wait_bytes(group_in, gr_recv)
        total = group_sum[y]
        for j in range(len(GROUP)):
            total += group_in[j]
        inverse = (1.0 / jnp.maximum(total[0:4], 1.0))[:, None, :]

        def reduce_start(inst, s):
            copies = []
            for k in range(1, 4):
                there = lax.rem(y + k, 4)
                copies.append(
                    remote(
                        part.at[s, pl.ds(there * 4, 4)], rs_in.at[inst, s, k - 1],
                        rs_send.at[inst, s], rs_recv.at[inst, s], (0, 0, k, 0),
                    )
                )
            for copy in copies:
                copy.start()

        def reduce_end(inst, s):
            wait_bytes(rs_in.at[inst, s], rs_recv.at[inst, s])
            total = part[s, pl.ds(y * 4, 4)] + rs_in[inst, s, 0] + rs_in[inst, s, 1] + rs_in[inst, s, 2]
            wait_bytes(rs_in.at[inst, s], rs_send.at[inst, s])
            return total

        lt_copy.wait_recv()
        for s in range(STREAMS):
            at = pl.multiple_of(core * 32 + s * 16, 16)
            part[s] = lt[:, pl.ds(at, 16), :] + lt_in[:, s * 16 : s * 16 + 16]
            reduce_start(0, s)

        wait_bytes(mass_in, ms_recv)
        total = mass_own[...]
        for j in range(len(PLANE)):
            total += mass_in[j]
        mass_sum[...] = total
        for copy in total_copies:
            copy.start()

        lt_copy.wait_send()
        wait_bytes(group_in, gr_send)
        wait_bytes(mass_in, ms_send)
        topic = [reduce_end(0, s) for s in range(STREAMS)]
        wait_bytes(mass_all, mg_recv)
        total = mass_sum[...]
        for j in range(len(GROUP)):
            total += mass_all[j]
        square = jnp.transpose(jnp.broadcast_to(total[0:1], (128, 128)))
        mass = jnp.where(core == 0, square[0:32], square[32:64])
        member = tel_ref[pl.ds(y * 4, 4), :].astype(jnp.float32)[:, None, :]
        for s in range(STREAMS):
            start = member * topic[s] / mass[None, s * 16 : s * 16 + 16]
            tele[s] = start
            state[s] = start
        wait_bytes(mass_all, mg_send)
        meta_own.wait()
        meta_local.wait()
        tile_copy.wait()

        def along(axis, k):
            return tuple(k if axis == name else 0 for name in "zxy") + (0,)

        class Stream:
            def __init__(self, hop, s, gathered):
                self.hop, self.s, self.gathered = hop, s, gathered

            def place(self, fixed, first, count):
                index = [fixed[axis] if axis in fixed else slice(None) for axis in "zxy"]
                return self.gathered.at[(*index, pl.ds(first, count))]

            def send(self, slot, axis, k, ref):
                at = (self.hop, self.s)
                copy = remote(ref, ref, ag_send.at[at], ag_recv.at[(*at, slot)], along(axis, k))
                copy.start()
                return copy

            def stage1(self):
                sent = (state[self.s] * inverse).astype(jnp.bfloat16)
                self.gathered[pos["z"], pos["x"], y] = sent
                for o, (a1, a2, a3, first, count) in enumerate(ORDERS[self.s]):
                    ref = self.place(pos, first, count)
                    for k in range(1, 4):
                        self.send(o, a1, k, ref)

            def stage2(self):
                self.two = []
                for o, (a1, a2, a3, first, count) in enumerate(ORDERS[self.s]):
                    wait_bytes(self.gathered.at[0, 0, pl.ds(0, 3), pl.ds(0, count)], ag_recv.at[self.hop, self.s, o])
                    ref = self.place({a2: pos[a2], a3: pos[a3]}, first, count)
                    self.two.append([self.send(3 * o + 2 + k, a2, k, ref) for k in range(1, 4)])
                    for k in range(1, 4):
                        self.send(12, a3, k, ref)

            def stage3(self):
                for k2 in (1, 3, 2):
                    for o, (a1, a2, a3, first, count) in enumerate(ORDERS[self.s]):
                        self.two[o][k2 - 1].wait_recv()
                        there = lax.rem(pos[a2] + 4 - k2, 4)
                        ref = self.place({a2: there, a3: pos[a3]}, first, count)
                        for k in range(1, 4):
                            self.send(12, a3, k, ref)

            def multiply(self):
                wait_bytes(runs.at[:, pl.ds(0, 48)], ag_recv.at[self.hop, self.s, 12])
                lists = ((own_smem, own_tiles), (sib_smem, sib_tiles))
                batch = 32
                gathered, s = self.gathered, self.s

                def tile_body(i, run):
                    run = list(run)
                    for j in range(batch):
                        r = i * batch + j
                        for n, (m, t) in enumerate(lists):
                            b = m[1, r]
                            slab = gathered[b // 64, (b // 16) % 4, (b // 4) % 4, b % 4]
                            prod = lax.dot_general(slab, t[m[0, r]], NT, preferred_element_type=jnp.float32)
                            run[n] = jnp.where(m[2, r] > 0, run[n], 0.0) + prod
                            runs[n, r] = run[n]
                    return tuple(run)

                zero = jnp.zeros((16, 128), jnp.float32)
                lax.fori_loop(0, own_tiles.shape[0] // batch, tile_body, (zero, zero))
                for blk in range(16):
                    value = zero
                    for n, (m, t) in enumerate(lists):
                        value += jnp.where(m[4, blk] > 0, runs[n, m[3, blk]], 0.0)
                    part[s, blk] = value
                reduce_start(self.hop + 1, s)

            def finish(self):
                inflow = reduce_end(self.hop + 1, self.s)
                state[self.s] = 0.85 * inflow + 0.15 * tele[self.s]

            def settle(self):
                wait_bytes(runs.at[:, pl.ds(0, 63)], ag_send.at[self.hop, self.s])

        streams = [[Stream(hop, s, g) for s, g in enumerate(gs)] for hop, gs in enumerate(((g00, g01), (g10, g11), (g20, g21)))]
        for one in streams[0]:
            one.stage1()
        for hop in range(HOPS):
            for one in streams[hop]:
                one.stage2()
            for one in streams[hop]:
                one.stage3()
            for one in streams[hop]:
                one.multiply()
            for s, one in enumerate(streams[hop]):
                one.finish()
                if hop + 1 < HOPS:
                    streams[hop + 1][s].stage1()
            for one in streams[hop]:
                one.settle()

        hosts_all = 128.0 * 256.0
        keep = pl.multiple_of(core * 2, 2)
        give = pl.multiple_of(2 - core * 2, 2)
        state[...] = hosts_all * state[...]
        last = remote(state.at[:, pl.ds(give, 2)], final.at[core], sib_send.at[3], sib_recv.at[3], SIBLING)
        last.start()
        final[core] = state[:, pl.ds(keep, 2)]
        last.wait()
        for j in range(2):
            out_ref[j * 128 : (j + 1) * 128, :] = jnp.transpose(final[:, :, j].reshape(64, 128))


def body(docs, w_in, w_out, doc_host, tiles, dst_block, src_block, tile_count, teleport):
    f32, bf16, i32 = jnp.float32, jnp.bfloat16, jnp.int32
    docs_dev, depth = docs.shape
    hidden, topics = w_out.shape
    slots = tiles.shape[0]
    steps = 8
    rows = docs_dev // steps

    def whole(*shape):
        return pl.BlockSpec(shape, lambda i: (0,) * len(shape))

    dma = pltpu.SemaphoreType.DMA
    return pl.pallas_call(
        kernel,
        grid=(steps,),
        out_shape=jax.ShapeDtypeStruct((256, topics), f32),
        in_specs=[
            pl.BlockSpec(memory_space=pltpu.SMEM),
            whole(1, slots),
            whole(1, slots),
            pl.BlockSpec((rows, depth), lambda i: (i, 0)),
            whole(depth, hidden),
            whole(topics, hidden),
            pl.BlockSpec((1, 1, rows), lambda i: (i, 0, 0)),
            whole(16, 128),
            pl.BlockSpec(memory_space=pl.ANY),
        ],
        out_specs=whole(256, topics),
        scratch_shapes=[
            pltpu.VMEM((1024, 256), f32),
            pltpu.VMEM((16, topics, 128), f32),
            pltpu.VMEM((8, 128), i32),
            pltpu.VMEM((8, 128), i32),
            pltpu.SMEM((8, 128), i32),
            pltpu.VMEM((8, 128), i32),
            pltpu.SMEM((8, 128), i32),
            pltpu.VMEM(tiles.shape, bf16),
            pltpu.VMEM(tiles.shape, bf16),
            pltpu.VMEM((16, 32, 128), f32),
            pltpu.VMEM((16, 4, 8, 128), f32),
            pltpu.VMEM((15, 4, 8, 128), f32),
            pltpu.VMEM((4, 8, 128), f32),
            pltpu.VMEM((7, 8, 128), f32),
            pltpu.VMEM((8, 128), f32),
            pltpu.VMEM((15, 8, 128), f32),
            pltpu.VMEM((8, 128), f32),
            pltpu.VMEM((7, 8, 128), f32),
            pltpu.VMEM((STREAMS, 16, 16, 128), f32),
            pltpu.VMEM((HOPS + 1, STREAMS, 3, 4, 16, 128), f32),
            pltpu.VMEM((STREAMS, 4, 16, 128), f32),
            pltpu.VMEM((STREAMS, 4, 16, 128), f32),
            *[pltpu.VMEM((4, 4, 4, 4, 16, 128), bf16) for _ in range(HOPS * STREAMS)],
            pltpu.VMEM((2, slots, 16, 128), f32),
            pltpu.VMEM((2, STREAMS, 2, 16, 128), f32),
            dma((3,)), dma((4,)), dma((4,)), *[dma] * 8,
            dma((HOPS + 1, STREAMS)), dma((HOPS + 1, STREAMS)), dma((HOPS, STREAMS)), dma((HOPS, STREAMS, 13)),
        ],
        compiler_params=pltpu.CompilerParams(
            collective_id=0, has_side_effects=True, vmem_limit_bytes=58 << 20
        ),
        name="spread",
    )(
        tile_count, dst_block.reshape(1, slots), src_block.reshape(1, slots), docs, w_in, w_out.T,
        doc_host.reshape(steps, 1, rows), teleport.reshape(16, 128), tiles,
    )


def solution(mesh):
    placed = (
        P(("hst", "doc"), None),
        P(),
        P(),
        P(("hst", "doc")),
        P(("hst", "doc"), None, None),
        P(("hst", "doc")),
        P(("hst", "doc")),
        P(("hst", "doc")),
        P("hst"),
    )
    return jax.shard_map(
        body, mesh=mesh, in_specs=placed, out_specs=P(("hst", "doc"), None), check_vma=False
    )
```

time: 641 us -> 108 us (0.17)
  waiting for transfers between devices: 477 us -> 0 us
  Pallas kernels: 0 us -> 105 us
  other arithmetic: 58.8 us -> 0 us
  blocking collectives: 33.5 us -> 0 us
  local copies, waits for them, and re-layouts: 33.6 us -> 1.62 us
  matrix products: 21.7 us -> 0 us
  between operations: 14.4 us -> 0.66 us
    psum x5 -> x0, waiting for transfers between devices: 317 us -> none  [the longest x3 175 us: body(): inflow = lax.psum(gathered.reshape(host_dev, topics), 'doc')]
    all_gather x3 -> x0, waiting for transfers between devices: 160 us -> none  [body(): full = lax.all_gather(sent, 'hst', axis=0, tiled=True)]
    pallas_call x0 -> x1, Pallas kernels: none -> 105 us  [body(): pl.pallas_call(kernel, grid=(steps,), out_shape=jax.ShapeDtypeStruct((256...]
    scatter-add x1 -> x0, other arithmetic: 44.5 us -> none  [body(): local_topic = jax.ops.segment_sum(probs, doc_host, num_segments=host_dev)]
    psum x1 -> x0, blocking collectives: 33.5 us -> none  [body(): mass = lax.psum(jnp.sum(member[:, None] * host_topic, axis=0), 'hst')]
    dot_general x8 -> x0, matrix products: 21.7 us -> none  [the longest x1 8.63 us: body(): jnp.dot(hidden, w_out, preferred_element_type=jnp.float32)]
    reshape x3 -> x0, local copies, waits for them, and re-layouts: 16.1 us -> none  [body(): slabs = full.reshape(nblocks, block, topics)[src_block]]
    gather x3 -> x0, local copies, waits for them, and re-layouts: 9.33 us -> none  [body(): slabs = full.reshape(nblocks, block, topics)[src_block]]
  transfers between devices with their start and end apart: 8 -> 0, of which waited for: 8 -> 0; matrix products, arithmetic and copies ran while one was open for 9% -> 0% of each run, Pallas kernels for 0% -> 0%
where the time goes in v3:
time: 108 us
  Pallas kernels  105 us (97%)
  local copies, waits for them, and re-layouts  1.62 us (2%)
    pallas_call x1, Pallas kernels, body(): pl.pallas_call(kernel, grid=(steps,), out_shape=jax.ShapeDtypeStruct((256...  105 us

profile of v3, /device:TPU:1, one launch (start us, length us, event | category | flops | bytes accessed | tf_op | source)
XLA Modules:
  0.0 107.6 jit_solution(13144448686336414862)
XLA Ops:
  0.7 105.4 %spread.1 = f32[256,64]{1,0:T(8,128)} custom-call(s32[1]{0:T(128)S(6)} %copy.11.cnt_ref, s32[1,64]{1,0:T(1,128)} %bitcast.8, s32[1,64]{1,0:T(1,128)} %bitcast.9, bf16[8192,768]{1,0:T(8,128)(2,1)} %docs_ref.1, bf16[768,256]{1,0:T(8,128)(2,1)} %win_ref.1, bf16[64,256]{1,0:T(8,128)(2,1)} %bitcast.5, s32[8,1,1024]{2,1,0:T(1,128)} %bitcast.6, s32[16,128]{1,0:T(8,128)} %bitcast.7, ...), custom_call_target="tpu_custom_call" | custom-call | tf_op jit(solution)/shard_map/spread/pallas_call | solution.py:374
  106.0 1.6 %copy.10 = f32[256,64]{0,1:T(8,128)} copy(f32[256,64]{1,0:T(8,128)} %spread.1) | data formatting | bytes 131072 | tf_op jit(solution)/shard_map/spread/pallas_call | solution.py:374

commit v4 on v3

--- a/solution.py
+++ b/solution.py
@@ -73,7 +73,7 @@
 
 def kernel(
     cnt_ref, dst_ref, src_ref, docs_ref, win_ref, wout_ref, dh_ref, tel_ref, tiles_any, out_ref,
-    acc, lt, rows, meta, own_smem, sib_meta, sib_smem, own_tiles, sib_tiles, lt_in, stage, stage_in,
+    acc, lt, rows, meta, own_smem, sib_meta, sib_smem, raw_tiles, own_tiles, sib_tiles, lt_in, stage, stage_in,
     group_sum, group_in, mass_own, mass_in, mass_sum, mass_all, part, rs_in,
     tele, state, g00, g01, g10, g11, g20, g21, runs, final,
     loc_sem, sib_send, sib_recv, st_send, st_recv, gr_send, gr_recv,
@@ -96,7 +96,7 @@
     def wait_bytes(ref, sem):
         pltpu.make_async_copy(ref, ref, sem).wait()
 
-    own_copy = pltpu.make_async_copy(tiles_any, own_tiles, loc_sem.at[0])
+    own_copy = pltpu.make_async_copy(tiles_any, raw_tiles, loc_sem.at[0])
     meta_own = pltpu.make_async_copy(meta, own_smem, loc_sem.at[1])
     meta_local = pltpu.make_async_copy(sib_meta, sib_smem, loc_sem.at[2])
     meta_copy = remote(meta, sib_meta, sib_send.at[1], sib_recv.at[1], SIBLING)
@@ -116,6 +116,14 @@
         remote(mass_sum, mass_all.at[j], mg_send, mg_recv, to) for j, to in enumerate(GROUP)
     ]
 
+    def flip_tiles():
+        def flip(i, carry):
+            for j in range(8):
+                own_tiles[i * 8 + j] = jnp.transpose(raw_tiles[i * 8 + j])
+            return carry
+
+        lax.fori_loop(0, own_tiles.shape[0] // 8, flip, 0)
+
     @pl.when(step == 0)
     def _():
         barrier = pltpu.get_barrier_semaphore()
@@ -125,7 +133,11 @@
         acc[...] = jnp.zeros_like(acc)
         order_tiles(dst_ref, src_ref, cnt_ref[0], rows, meta)
         meta_own.start()
+
+    @pl.when(step == 1)
+    def _():
         own_copy.wait()
+        flip_tiles()
 
     @pl.when(step == 2)
     def _():
@@ -133,7 +145,7 @@
         meta_copy.start()
         tile_copy.start()
         slots = own_tiles.shape[0]
-        colsum = jnp.sum(own_tiles[...].astype(jnp.float32), axis=1)
+        colsum = jnp.sum(raw_tiles[...].astype(jnp.float32), axis=1)
         row = lax.broadcasted_iota(jnp.int32, (512, slots), 0)
         src = src_ref[...]
         used = lax.broadcasted_iota(jnp.int32, (1, slots), 1) < cnt_ref[0]
@@ -299,7 +311,7 @@
             def multiply(self):
                 wait_bytes(runs.at[:, pl.ds(0, 48)], ag_recv.at[self.hop, self.s, 12])
                 lists = ((own_smem, own_tiles), (sib_smem, sib_tiles))
-                batch = 32
+                batch = 64
                 gathered, s = self.gathered, self.s
 
                 def tile_body(i, run):
@@ -308,8 +320,8 @@
                         r = i * batch + j
                         for n, (m, t) in enumerate(lists):
                             b = m[1, r]
-                            slab = gathered[b // 64, (b // 16) % 4, (b // 4) % 4, b % 4]
-                            prod = lax.dot_general(slab, t[m[0, r]], NT, preferred_element_type=jnp.float32)
+                            slab = gathered[b >> 6, (b >> 4) & 3, (b >> 2) & 3, b & 3]
+                            prod = jnp.dot(slab, t[m[0, r]], preferred_element_type=jnp.float32)
                             run[n] = jnp.where(m[2, r] > 0, run[n], 0.0) + prod
                             runs[n, r] = run[n]
                     return tuple(run)
@@ -395,6 +407,7 @@
             pltpu.SMEM((8, 128), i32),
             pltpu.VMEM((8, 128), i32),
             pltpu.SMEM((8, 128), i32),
+            pltpu.VMEM(tiles.shape, bf16),
             pltpu.VMEM(tiles.shape, bf16),
             pltpu.VMEM(tiles.shape, bf16),
             pltpu.VMEM((16, 32, 128), f32),

time: 108 us -> 100 us (0.926)
  Pallas kernels: 105 us -> 97.6 us
    pallas_call x1, Pallas kernels: 105 us -> 97.6 us  [body(): pl.pallas_call(kernel, grid=(steps,), out_shape=jax.ShapeDtypeStruct((256...]
where the time goes in v4:
time: 100 us; the launch traced here: 99.8 us
  Pallas kernels  97.6 us (98%)
  local copies, waits for them, and re-layouts  1.62 us (2%)
    pallas_call x1, Pallas kernels, body(): pl.pallas_call(kernel, grid=(steps,), out_shape=jax.ShapeDtypeStruct((256...  97.6 us

profile of v4, /device:TPU:1, one launch (start us, length us, event | category | flops | bytes accessed | tf_op | source)
XLA Modules:
  0.0 99.8 jit_solution(16379974753580556042)
XLA Ops:
  0.7 97.6 %spread.1 = f32[256,64]{1,0:T(8,128)} custom-call(s32[1]{0:T(128)S(6)} %copy.11.cnt_ref, s32[1,64]{1,0:T(1,128)} %bitcast.8, s32[1,64]{1,0:T(1,128)} %bitcast.9, bf16[8192,768]{1,0:T(8,128)(2,1)} %docs_ref.1, bf16[768,256]{1,0:T(8,128)(2,1)} %win_ref.1, bf16[64,256]{1,0:T(8,128)(2,1)} %bitcast.5, s32[8,1,1024]{2,1,0:T(1,128)} %bitcast.6, s32[16,128]{1,0:T(8,128)} %bitcast.7, ...), custom_call_target="tpu_custom_call" | custom-call | tf_op jit(solution)/shard_map/spread/pallas_call | solution.py:386
  98.2 1.6 %copy.10 = f32[256,64]{0,1:T(8,128)} copy(f32[256,64]{1,0:T(8,128)} %spread.1) | data formatting | bytes 131072 | tf_op jit(solution)/shard_map/spread/pallas_call | solution.py:386

commit v5 on v4

--- a/solution.py
+++ b/solution.py
@@ -23,6 +23,7 @@
 GROUP = [(0, 0, y, c) for y in range(4) for c in range(2) if y or c]
 SIBLING = (0, 0, 0, 1)
 STREAMS = 2
+FAR = (2, 1, 3)
 ORDERS = (
     (("x", "z", "y", 0, 1), ("z", "y", "x", 1, 2), ("y", "x", "z", 3, 1)),
     (("x", "z", "y", 0, 1), ("z", "y", "x", 1, 1), ("y", "x", "z", 2, 2)),
@@ -179,7 +180,7 @@
         ).astype(jnp.bfloat16)
         logits = lax.dot_general(wout_ref[...], hidden, NT, preferred_element_type=jnp.float32)
         weight = jnp.exp(logits - jnp.max(logits, axis=0, keepdims=True))
-        probs = weight / jnp.sum(weight, axis=0, keepdims=True)
+        probs = weight * (1.0 / jnp.sum(weight, axis=0, keepdims=True))
         high = probs.astype(jnp.bfloat16)
         low = (probs - high.astype(jnp.float32)).astype(jnp.bfloat16)
         both = jnp.concatenate([high, low], axis=0)
@@ -188,8 +189,8 @@
     spot = (owner & 1023)
     piece = 512
     for at in range(0, 1024, piece):
-        row = (lax.broadcasted_iota(jnp.int32, (piece, owner.shape[1]), 0) + at)
-        onehot = jnp.where(row == spot, 1.0, 0.0).astype(jnp.bfloat16)
+        row = lax.broadcasted_iota(jnp.int32, (piece, owner.shape[1]), 0)
+        onehot = jnp.where(row == spot - at, 1.0, 0.0).astype(jnp.bfloat16)
         acc[at : at + piece] += lax.dot_general(onehot, pt, NT, preferred_element_type=jnp.float32)
 
     @pl.when(step == pl.num_programs(0) - 1)
@@ -214,7 +215,7 @@
 
         def reduce_start(inst, s):
             copies = []
-            for k in range(1, 4):
+            for k in FAR:
                 there = lax.rem(y + k, 4)
                 copies.append(
                     remote(
@@ -287,25 +288,27 @@
                 self.gathered[pos["z"], pos["x"], y] = sent
                 for o, (a1, a2, a3, first, count) in enumerate(ORDERS[self.s]):
                     ref = self.place(pos, first, count)
-                    for k in range(1, 4):
+                    for k in FAR:
                         self.send(o, a1, k, ref)
 
             def stage2(self):
-                self.two = []
+                self.two, later = [], []
                 for o, (a1, a2, a3, first, count) in enumerate(ORDERS[self.s]):
                     wait_bytes(self.gathered.at[0, 0, pl.ds(0, 3), pl.ds(0, count)], ag_recv.at[self.hop, self.s, o])
                     ref = self.place({a2: pos[a2], a3: pos[a3]}, first, count)
-                    self.two.append([self.send(3 * o + 2 + k, a2, k, ref) for k in range(1, 4)])
-                    for k in range(1, 4):
+                    self.two.append({k: self.send(3 * o + 2 + k, a2, k, ref) for k in FAR})
+                    later.append((a3, ref))
+                for a3, ref in later:
+                    for k in FAR:
                         self.send(12, a3, k, ref)
 
             def stage3(self):
                 for k2 in (1, 3, 2):
                     for o, (a1, a2, a3, first, count) in enumerate(ORDERS[self.s]):
-                        self.two[o][k2 - 1].wait_recv()
+                        self.two[o][k2].wait_recv()
                         there = lax.rem(pos[a2] + 4 - k2, 4)
                         ref = self.place({a2: there, a3: pos[a3]}, first, count)
-                        for k in range(1, 4):
+                        for k in FAR:
                             self.send(12, a3, k, ref)
 
             def multiply(self):

time: 100 us -> 98.5 us (0.985)
  Pallas kernels: 97.6 us -> 96.1 us
    pallas_call x1, Pallas kernels: 97.6 us -> 96.1 us  [body(): pl.pallas_call(kernel, grid=(steps,), out_shape=jax.ShapeDtypeStruct((256...]
where the time goes in v5:
time: 98.5 us; the launch traced here: 98.4 us
  Pallas kernels  96.1 us (98%)
  local copies, waits for them, and re-layouts  1.62 us (2%)
    pallas_call x1, Pallas kernels, body(): pl.pallas_call(kernel, grid=(steps,), out_shape=jax.ShapeDtypeStruct((256...  96.1 us

profile of v5, /device:TPU:1, one launch (start us, length us, event | category | flops | bytes accessed | tf_op | source)
XLA Modules:
  0.0 98.4 jit_solution(7380491915670555542)
XLA Ops:
  0.7 96.1 %spread.1 = f32[256,64]{1,0:T(8,128)} custom-call(s32[1]{0:T(128)S(6)} %copy.11.cnt_ref, s32[1,64]{1,0:T(1,128)} %bitcast.8, s32[1,64]{1,0:T(1,128)} %bitcast.9, bf16[8192,768]{1,0:T(8,128)(2,1)} %docs_ref.1, bf16[768,256]{1,0:T(8,128)(2,1)} %win_ref.1, bf16[64,256]{1,0:T(8,128)(2,1)} %bitcast.5, s32[8,1,1024]{2,1,0:T(1,128)} %bitcast.6, s32[16,128]{1,0:T(8,128)} %bitcast.7, ...), custom_call_target="tpu_custom_call" | custom-call | tf_op jit(solution)/shard_map/spread/pallas_call | solution.py:389
  96.8 1.6 %copy.10 = f32[256,64]{0,1:T(8,128)} copy(f32[256,64]{1,0:T(8,128)} %spread.1) | data formatting | bytes 131072 | tf_op jit(solution)/shard_map/spread/pallas_call | solution.py:389

commit v6 on v5

--- a/solution.py
+++ b/solution.py
@@ -73,7 +73,7 @@
 
 
 def kernel(
-    cnt_ref, dst_ref, src_ref, docs_ref, win_ref, wout_ref, dh_ref, tel_ref, tiles_any, out_ref,
+    cnt_ref, dst_ref, src_ref, docs_ref, win_ref, wout_ref, dh_ref, tel_ref, tiles_ref, tiles_any, out_ref,
     acc, lt, rows, meta, own_smem, sib_meta, sib_smem, raw_tiles, own_tiles, sib_tiles, lt_in, stage, stage_in,
     group_sum, group_in, mass_own, mass_in, mass_sum, mass_all, part, rs_in,
     tele, state, g00, g01, g10, g11, g20, g21, runs, final,
@@ -117,14 +117,6 @@
         remote(mass_sum, mass_all.at[j], mg_send, mg_recv, to) for j, to in enumerate(GROUP)
     ]
 
-    def flip_tiles():
-        def flip(i, carry):
-            for j in range(8):
-                own_tiles[i * 8 + j] = jnp.transpose(raw_tiles[i * 8 + j])
-            return carry
-
-        lax.fori_loop(0, own_tiles.shape[0] // 8, flip, 0)
-
     @pl.when(step == 0)
     def _():
         barrier = pltpu.get_barrier_semaphore()
@@ -135,17 +127,12 @@
         order_tiles(dst_ref, src_ref, cnt_ref[0], rows, meta)
         meta_own.start()
 
-    @pl.when(step == 1)
-    def _():
-        own_copy.wait()
-        flip_tiles()
-
     @pl.when(step == 2)
     def _():
         pl.semaphore_wait(pltpu.get_barrier_semaphore(), len(PLANE) + len(GROUP))
         meta_copy.start()
-        tile_copy.start()
-        slots = own_tiles.shape[0]
+        own_copy.wait()
+        slots = raw_tiles.shape[0]
         colsum = jnp.sum(raw_tiles[...].astype(jnp.float32), axis=1)
         row = lax.broadcasted_iota(jnp.int32, (512, slots), 0)
         src = src_ref[...]
@@ -186,6 +173,8 @@
         both = jnp.concatenate([high, low], axis=0)
         pts.append(jnp.concatenate([both * lower[:, c:c+1024], both * upper[:, c:c+1024]], axis=0))
     pt = jnp.concatenate(pts, axis=1)
+    for j in range(tiles_ref.shape[0]):
+        own_tiles[step * tiles_ref.shape[0] + j] = jnp.transpose(tiles_ref[j])
     spot = (owner & 1023)
     piece = 512
     for at in range(0, 1024, piece):
@@ -207,6 +196,7 @@
         mass_own[...] = jnp.broadcast_to(jnp.sum(jnp.transpose(wide), axis=0, keepdims=True), (8, 128))
         for copy in mass_copies:
             copy.start()
+        tile_copy.start()
         wait_bytes(group_in, gr_recv)
         total = group_sum[y]
         for j in range(len(GROUP)):
@@ -399,6 +389,7 @@
             whole(topics, hidden),
             pl.BlockSpec((1, 1, rows), lambda i: (i, 0, 0)),
             whole(16, 128),
+            pl.BlockSpec((slots // steps, 128, 128), lambda i: (i, 0, 0)),
             pl.BlockSpec(memory_space=pl.ANY),
         ],
         out_specs=whole(256, topics),
@@ -438,7 +429,7 @@
         name="spread",
     )(
         tile_count, dst_block.reshape(1, slots), src_block.reshape(1, slots), docs, w_in, w_out.T,
-        doc_host.reshape(steps, 1, rows), teleport.reshape(16, 128), tiles,
+        doc_host.reshape(steps, 1, rows), teleport.reshape(16, 128), tiles, tiles,
     )
 
 

time: 98.5 us -> 97.7 us (level)
  no operation moved by 1% of the time
where the time goes in v6:
time: 97.7 us; the launch traced here: 97.5 us
  Pallas kernels  95.3 us (98%)
  local copies, waits for them, and re-layouts  1.62 us (2%)
    pallas_call x1, Pallas kernels, body(): pl.pallas_call(kernel, grid=(steps,), out_shape=jax.ShapeDtypeStruct((256...  95.3 us

profile of v6, /device:TPU:1, one launch (start us, length us, event | category | flops | bytes accessed | tf_op | source)
XLA Modules:
  0.0 97.5 jit_solution(10639703332885770067)
XLA Ops:
  0.7 95.3 %spread.1 = f32[256,64]{1,0:T(8,128)} custom-call(s32[1]{0:T(128)S(6)} %copy.11.cnt_ref, s32[1,64]{1,0:T(1,128)} %bitcast.8, s32[1,64]{1,0:T(1,128)} %bitcast.9, bf16[8192,768]{1,0:T(8,128)(2,1)} %docs_ref.1, bf16[768,256]{1,0:T(8,128)(2,1)} %win_ref.1, bf16[64,256]{1,0:T(8,128)(2,1)} %bitcast.5, s32[8,1,1024]{2,1,0:T(1,128)} %bitcast.6, s32[16,128]{1,0:T(8,128)} %bitcast.7, ...), custom_call_target="tpu_custom_call" | custom-call | tf_op jit(solution)/shard_map/spread/pallas_call | solution.py:379
  95.9 1.6 %copy.10 = f32[256,64]{0,1:T(8,128)} copy(f32[256,64]{1,0:T(8,128)} %spread.1) | data formatting | bytes 131072 | tf_op jit(solution)/shard_map/spread/pallas_call | solution.py:379
